TPU v7x, 32 devices: a whole 2x2x4 slice. The times are simulated.
32 devices in a mesh: dp: 16 (over z, y, core), blk: 2 (over x).
Axes of the slice: x: 2, y: 2, z: 4, core: 2. Of those that a mesh axis runs over, the one named last changes fastest.
Arguments:
- hidden_in: bfloat16 [8192, 768], P(('dp', 'blk')), may hold values from -6 to 6
- cotangent: bfloat16 [8192, 768], P(('dp', 'blk')), may hold values from -6 to 6
- lengths: int32 [16], P('dp'), may hold values from 320 to 480, as said below
- coords: int32 [2, 8192], P(None, ('dp', 'blk')), may hold values from 0 to 1000
- qkv_weight: bfloat16 [2, 768, 2304], P(None, ('dp', 'blk')), may hold values from -0.21875 to 0.21875
- query_bias: bfloat16 [2, 768], P(None, ('dp', 'blk')), may hold values from -3 to 3
- value_bias: bfloat16 [2, 768], P(None, ('dp', 'blk')), may hold values from -3 to 3
- out_weight: bfloat16 [2, 768, 768], P(None, ('dp', 'blk')), may hold values from -1.25 to 1.25
- out_bias: bfloat16 [2, 768], P(None, ('dp', 'blk')), may hold values from -3 to 3
- norm1_gain: bfloat16 [2, 768], P(None, ('dp', 'blk')), may hold values from 0.099609375 to 1.8984375
- norm1_shift: bfloat16 [2, 768], P(None, ('dp', 'blk')), may hold values from -2 to 2
- in_weight: bfloat16 [2, 768, 3072], P(None, ('dp', 'blk')), may hold values from -0.21875 to 0.21875
- in_bias: bfloat16 [2, 3072], P(None, ('dp', 'blk')), may hold values from -3 to 3
- back_weight: bfloat16 [2, 3072, 768], P(None, ('dp', 'blk')), may hold values from -0.109375 to 0.109375
- back_bias: bfloat16 [2, 768], P(None, ('dp', 'blk')), may hold values from -3 to 3
- norm2_gain: bfloat16 [2, 768], P(None, ('dp', 'blk')), may hold values from 0.099609375 to 1.8984375
- norm2_shift: bfloat16 [2, 768], P(None, ('dp', 'blk')), may hold values from -2 to 2
- line_table: bfloat16 [32, 12], replicated, may hold values from -3 to 3
- horizontal_table: bfloat16 [64, 12], replicated, may hold values from -3 to 3
- vertical_table: bfloat16 [64, 12], replicated, may hold values from -3 to 3
Outputs:
- hidden_out: bfloat16 [8192, 768], P(('dp', 'blk'))
- grad_in: bfloat16 [8192, 768], P(('dp', 'blk'))
- grad_qkv_weight: float32 [2, 768, 2304], P(None, ('dp', 'blk'))
- grad_query_bias: float32 [2, 768], P(None, ('dp', 'blk'))
- grad_value_bias: float32 [2, 768], P(None, ('dp', 'blk'))
- grad_out_weight: float32 [2, 768, 768], P(None, ('dp', 'blk'))
- grad_out_bias: float32 [2, 768], P(None, ('dp', 'blk'))
- grad_norm1_gain: float32 [2, 768], P(None, ('dp', 'blk'))
- grad_norm1_shift: float32 [2, 768], P(None, ('dp', 'blk'))
- grad_in_weight: float32 [2, 768, 3072], P(None, ('dp', 'blk'))
- grad_in_bias: float32 [2, 3072], P(None, ('dp', 'blk'))
- grad_back_weight: float32 [2, 3072, 768], P(None, ('dp', 'blk'))
- grad_back_bias: float32 [2, 768], P(None, ('dp', 'blk'))
- grad_norm2_gain: float32 [2, 768], P(None, ('dp', 'blk'))
- grad_norm2_shift: float32 [2, 768], P(None, ('dp', 'blk'))
- grad_line_table: float32 [32, 12], replicated
- grad_horizontal_table: float32 [64, 12], replicated
- grad_vertical_table: float32 [64, 12], replicated
Inputs may be any that keep to these rules, and one draw needn't show every extreme that they name: `lengths`: each entry is the number of real tokens of the one document of a group; they are the first of the group's 512 slots and the rest are padding.
All inputs are finite; a program needn't handle non-finite values.
Results may differ from a plain program's by a relative error of at most 0.029.
Values may be sent and summed in bfloat16 or wider, within the bound.
No kernel may reach another device: no remote copies, remote signals or barrier semaphores. Data moves between devices by JAX's collectives and lax.ppermute only.
A program may use at most 256 MiB of HBM per device.

v0:
```python
import math

import jax
import jax.numpy as jnp
from jax import lax
from jax.sharding import PartitionSpec as P

REACH_1D = 128
REACH_2D = 256


eps_norm = 1e-12
big_negative = -1e30


def passed_along(block, axis, distance):
    devices = range(lax.axis_size(axis))
    route = [((i - distance) % len(devices), i) for i in devices]
    return lax.ppermute(block, axis, route)


def bucket_marks(bucket_count, far_reach):
    half_count = bucket_count // 2
    exact_limit = half_count // 2
    thresholds = []
    for bucket_step in range(1, half_count):
        if bucket_step < exact_limit:
            thresholds.append(bucket_step)
        else:
            thresholds.append(
                math.ceil(
                    exact_limit
                    * (far_reach / exact_limit)
                    ** ((bucket_step - exact_limit) / (half_count - exact_limit))
                )
            )
    return thresholds


def bucket_of(offset, bucket_count, far_reach):
    magnitude = jnp.abs(offset)
    result = jnp.where(offset > 0, bucket_count // 2, 0).astype(jnp.int32)
    for threshold in bucket_marks(bucket_count, far_reach):
        result = result + (magnitude >= threshold).astype(jnp.int32)
    return result


def layer_norm(values, gain, shift):
    centered = values - jnp.mean(values, axis=-1, keepdims=True)
    variance = jnp.mean(centered * centered, axis=-1, keepdims=True)
    return centered * lax.rsqrt(variance + eps_norm) * gain + shift


def gelu_exact(values):
    return jax.nn.gelu(values, approximate=False)


def over_rows(left, right):
    return lax.dot_general(
        left, right, (((0,), (0,)), ((), ())), preferred_element_type=jnp.float32
    )


def times_transposed(left, right):
    return lax.dot_general(
        left, right, (((1,), (1,)), ((), ())), preferred_element_type=jnp.float32
    )


def biased_scores(query_heads, all_keys, score_bias, same_doc):
    scores = (
        jnp.einsum("qhd,khd->hqk", query_heads, all_keys, preferred_element_type=jnp.float32)
        + score_bias
    )
    return jnp.where(same_doc[None], scores, big_negative)


def table_lookup(codes, column):
    code_range = jnp.arange(column.shape[0], dtype=jnp.int32)
    return jnp.sum(
        jnp.where(codes[None] == code_range[:, None, None], column[:, None, None], 0.0), axis=0
    )


def table_collect(codes, grad_plane, code_count):
    code_range = jnp.arange(code_count, dtype=jnp.int32)
    return jnp.sum(
        jnp.where(codes[None] == code_range[:, None, None], grad_plane[None], 0.0), axis=(1, 2)
    )


def forward_layer(state, weights, score_bias, same_doc, head_count):
    (
        qkv_weight,
        query_bias,
        value_bias,
        out_weight,
        out_bias,
        gain_one,
        shift_one,
        in_weight,
        in_bias,
        back_weight,
        back_bias,
        gain_two,
        shift_two,
    ) = weights
    tok_rows, model_width = state.shape
    head_dim = model_width // head_count
    inputs = state.astype(jnp.bfloat16)
    joined = jnp.dot(inputs, qkv_weight, preferred_element_type=jnp.float32)
    queries = ((joined[:, :model_width] + query_bias.astype(jnp.float32)) * 0.125).astype(
        jnp.bfloat16
    )
    keys = joined[:, model_width : 2 * model_width].astype(jnp.bfloat16)
    values = (joined[:, 2 * model_width :] + value_bias.astype(jnp.float32)).astype(jnp.bfloat16)
    query_heads = queries.reshape(tok_rows, head_count, head_dim)
    own_keys = keys.reshape(tok_rows, head_count, head_dim)
    own_values = values.reshape(tok_rows, head_count, head_dim)
    own_scores = biased_scores(
        query_heads, own_keys, score_bias[:, :, :tok_rows], same_doc[:, :tok_rows]
    )
    own_max = jnp.max(own_scores, axis=-1, keepdims=True)
    far_keys, far_values = passed_along((keys, values), "blk", 1)
    far_key_heads = far_keys.reshape(tok_rows, head_count, head_dim)
    far_value_heads = far_values.reshape(tok_rows, head_count, head_dim)
    far_scores = biased_scores(
        query_heads, far_key_heads, score_bias[:, :, tok_rows:], same_doc[:, tok_rows:]
    )
    row_max = jnp.maximum(own_max, jnp.max(far_scores, axis=-1, keepdims=True))
    own_lifted = jnp.exp(own_scores - row_max)
    far_lifted = jnp.exp(far_scores - row_max)
    row_total = jnp.sum(own_lifted, axis=-1, keepdims=True) + jnp.sum(
        far_lifted, axis=-1, keepdims=True
    )
    own_probs = (own_lifted / row_total).astype(jnp.bfloat16)
    far_probs = (far_lifted / row_total).astype(jnp.bfloat16)
    log_total = row_max + jnp.log(row_total)
    mixed = jnp.einsum(
        "hqk,khd->qhd", own_probs, own_values, preferred_element_type=jnp.float32
    ) + jnp.einsum("hqk,khd->qhd", far_probs, far_value_heads, preferred_element_type=jnp.float32)
    mixed = mixed.reshape(tok_rows, model_width).astype(jnp.bfloat16)
    attn_sum = (
        state
        + jnp.dot(mixed, out_weight, preferred_element_type=jnp.float32)
        + out_bias.astype(jnp.float32)
    )
    middle = layer_norm(attn_sum, gain_one.astype(jnp.float32), shift_one.astype(jnp.float32))
    middle_low = middle.astype(jnp.bfloat16)
    inner = jnp.dot(middle_low, in_weight, preferred_element_type=jnp.float32) + in_bias.astype(
        jnp.float32
    )
    active = gelu_exact(inner).astype(jnp.bfloat16)
    ffn_sum = (
        middle
        + jnp.dot(active, back_weight, preferred_element_type=jnp.float32)
        + back_bias.astype(jnp.float32)
    )
    new_state = layer_norm(ffn_sum, gain_two.astype(jnp.float32), shift_two.astype(jnp.float32))
    saved = (
        inputs,
        query_heads,
        keys,
        values,
        far_keys,
        far_values,
        log_total,
        mixed,
        attn_sum,
        middle_low,
        inner,
        active,
        ffn_sum,
    )
    return (new_state, saved)


def backward_layer(grad_state, weights, saved, far_pair, score_bias, same_doc, head_count):
    (
        qkv_weight,
        query_bias,
        value_bias,
        out_weight,
        out_bias,
        gain_one,
        shift_one,
        in_weight,
        in_bias,
        back_weight,
        back_bias,
        gain_two,
        shift_two,
    ) = weights
    (
        inputs,
        query_heads,
        keys,
        values,
        kept_keys,
        kept_values,
        log_total,
        mixed,
        attn_sum,
        middle_low,
        inner,
        active,
        ffn_sum,
    ) = saved
    far_keys, far_values = far_pair
    tok_rows, model_width = inputs.shape
    head_dim = model_width // head_count
    normed_two, pull_two = jax.vjp(
        layer_norm, ffn_sum, gain_two.astype(jnp.float32), shift_two.astype(jnp.float32)
    )
    grad_ffn, grad_gain_two, grad_shift_two = pull_two(grad_state)
    grad_back = grad_ffn.astype(jnp.bfloat16)
    grad_back_bias = jnp.sum(grad_back.astype(jnp.float32), axis=0)
    grad_back_weight = over_rows(active, grad_back)
    grad_active = times_transposed(grad_back, back_weight)
    gelu_value, pull_gelu = jax.vjp(gelu_exact, inner)
    grad_inner = pull_gelu(grad_active)[0].astype(jnp.bfloat16)
    grad_in_bias = jnp.sum(grad_inner.astype(jnp.float32), axis=0)
    grad_in_weight = over_rows(middle_low, grad_inner)
    grad_middle = grad_ffn + times_transposed(grad_inner, in_weight)
    normed_one, pull_one = jax.vjp(
        layer_norm, attn_sum, gain_one.astype(jnp.float32), shift_one.astype(jnp.float32)
    )
    grad_attn, grad_gain_one, grad_shift_one = pull_one(grad_middle)
    grad_branch = grad_attn.astype(jnp.bfloat16)
    grad_out_bias = jnp.sum(grad_branch.astype(jnp.float32), axis=0)
    grad_out_weight = over_rows(mixed, grad_branch)
    grad_mixed = (
        times_transposed(grad_branch, out_weight)
        .astype(jnp.bfloat16)
        .reshape(tok_rows, head_count, head_dim)
    )
    all_keys = jnp.concatenate([keys, far_keys], axis=0).reshape(2 * tok_rows, head_count, head_dim)
    all_values = jnp.concatenate([values, far_values], axis=0).reshape(
        2 * tok_rows, head_count, head_dim
    )
    scores = biased_scores(query_heads, all_keys, score_bias, same_doc)
    probs = jnp.exp(scores - log_total)
    grad_probs = jnp.einsum(
        "qhd,khd->hqk", grad_mixed, all_values, preferred_element_type=jnp.float32
    )
    inner_sum = jnp.sum(probs * grad_probs, axis=-1, keepdims=True)
    grad_scores = (probs * (grad_probs - inner_sum)).astype(jnp.bfloat16)
    grad_all_values = jnp.einsum(
        "hqk,qhd->khd", probs.astype(jnp.bfloat16), grad_mixed, preferred_element_type=jnp.float32
    ).reshape(2 * tok_rows, model_width)
    grad_all_keys = jnp.einsum(
        "hqk,qhd->khd", grad_scores, query_heads, preferred_element_type=jnp.float32
    ).reshape(2 * tok_rows, model_width)
    grad_queries = (
        jnp.einsum("hqk,khd->qhd", grad_scores, all_keys, preferred_element_type=jnp.float32)
        .reshape(tok_rows, model_width)
        .astype(jnp.bfloat16)
    )
    home_keys, home_values = (
        passed_along(grad_all_keys[tok_rows:].astype(jnp.bfloat16), "blk", 1).astype(jnp.float32),
        passed_along(grad_all_values[tok_rows:].astype(jnp.bfloat16), "blk", 1).astype(jnp.float32),
    )
    grad_keys = (grad_all_keys[:tok_rows] + home_keys).astype(jnp.bfloat16)
    grad_values = (grad_all_values[:tok_rows] + home_values).astype(jnp.bfloat16)
    grad_query_pre = (grad_queries.astype(jnp.float32) * 0.125).astype(jnp.bfloat16)
    grad_query_bias = jnp.sum(grad_query_pre.astype(jnp.float32), axis=0)
    grad_value_bias = jnp.sum(grad_values.astype(jnp.float32), axis=0)
    grad_joined = jnp.concatenate([grad_query_pre, grad_keys, grad_values], axis=1)
    grad_qkv_weight = over_rows(inputs, grad_joined)
    grad_prev = grad_attn + times_transposed(grad_joined, qkv_weight)
    grads = (
        grad_qkv_weight,
        grad_query_bias,
        grad_value_bias,
        grad_out_weight,
        grad_out_bias,
        grad_gain_one,
        grad_shift_one,
        grad_in_weight,
        grad_in_bias,
        grad_back_weight,
        grad_back_bias,
        grad_gain_two,
        grad_shift_two,
    )
    return (grad_prev, grads, grad_scores)


def on_device(
    hidden_in,
    cotangent,
    lengths,
    coords,
    qkv_weight,
    query_bias,
    value_bias,
    out_weight,
    out_bias,
    norm1_gain,
    norm1_shift,
    in_weight,
    in_bias,
    back_weight,
    back_bias,
    norm2_gain,
    norm2_shift,
    line_table,
    horizontal_table,
    vertical_table,
):
    tok_rows = hidden_in.shape[0]
    head_count = line_table.shape[1]
    line_count = line_table.shape[0]
    plane_count = horizontal_table.shape[0]
    layers = qkv_weight.shape[0]
    key_count = 2 * tok_rows
    cycle_place = lax.axis_index("blk")
    own_place = cycle_place * tok_rows + jnp.arange(tok_rows, dtype=jnp.int32)
    other_place = (1 - cycle_place) * tok_rows + jnp.arange(tok_rows, dtype=jnp.int32)
    key_place = jnp.concatenate([own_place, other_place])
    doc_length = lengths[0]
    same_doc = jnp.broadcast_to((key_place < doc_length)[None, :], (tok_rows, key_count))
    far_coords = passed_along(coords, "blk", 1)
    key_coords = jnp.concatenate([coords, far_coords], axis=1)
    bucket_line = bucket_of(key_place[None, :] - own_place[:, None], line_count, REACH_1D)
    bucket_across = bucket_of(key_coords[0][None, :] - coords[0][:, None], plane_count, REACH_2D)
    bucket_upward = bucket_of(key_coords[1][None, :] - coords[1][:, None], plane_count, REACH_2D)
    line_f = line_table.astype(jnp.float32)
    across_f = horizontal_table.astype(jnp.float32)
    upward_f = vertical_table.astype(jnp.float32)

    def head_bias(head):
        line_column = lax.dynamic_index_in_dim(line_f, head, 1, keepdims=False)
        across_column = lax.dynamic_index_in_dim(across_f, head, 1, keepdims=False)
        upward_column = lax.dynamic_index_in_dim(upward_f, head, 1, keepdims=False)
        return (
            table_lookup(bucket_line, line_column)
            + table_lookup(bucket_across, across_column)
            + table_lookup(bucket_upward, upward_column)
        )

    score_bias = lax.map(head_bias, jnp.arange(head_count, dtype=jnp.int32))
    all_weights = []
    all_saved = []
    state = hidden_in.astype(jnp.float32)
    for layer_index in range(layers):
        weights = (
            lax.all_gather(qkv_weight[layer_index], ("dp", "blk"), axis=0, tiled=True),
            lax.all_gather(query_bias[layer_index], ("dp", "blk"), axis=0, tiled=True),
            lax.all_gather(value_bias[layer_index], ("dp", "blk"), axis=0, tiled=True),
            lax.all_gather(out_weight[layer_index], ("dp", "blk"), axis=0, tiled=True),
            lax.all_gather(out_bias[layer_index], ("dp", "blk"), axis=0, tiled=True),
            lax.all_gather(norm1_gain[layer_index], ("dp", "blk"), axis=0, tiled=True),
            lax.all_gather(norm1_shift[layer_index], ("dp", "blk"), axis=0, tiled=True),
            lax.all_gather(in_weight[layer_index], ("dp", "blk"), axis=0, tiled=True),
            lax.all_gather(in_bias[layer_index], ("dp", "blk"), axis=0, tiled=True),
            lax.all_gather(back_weight[layer_index], ("dp", "blk"), axis=0, tiled=True),
            lax.all_gather(back_bias[layer_index], ("dp", "blk"), axis=0, tiled=True),
            lax.all_gather(norm2_gain[layer_index], ("dp", "blk"), axis=0, tiled=True),
            lax.all_gather(norm2_shift[layer_index], ("dp", "blk"), axis=0, tiled=True),
        )
        state, saved = forward_layer(state, weights, score_bias, same_doc, head_count)
        all_weights.append(weights)
        all_saved.append(saved)
    hidden_out = state.astype(jnp.bfloat16)
    real_rows = (own_place < doc_length).astype(jnp.float32)
    grad_state = cotangent.astype(jnp.float32) * real_rows[:, None]
    grad_shards = [None] * layers
    score_total = jnp.zeros((head_count, tok_rows, key_count), jnp.float32)
    for layer_index in reversed(range(layers)):
        saved = all_saved[layer_index]
        far_pair = (saved[4], saved[5])
        grad_state, grads, grad_scores = backward_layer(
            grad_state, all_weights[layer_index], saved, far_pair, score_bias, same_doc, head_count
        )
        score_total = score_total + grad_scores.astype(jnp.float32)
        grad_shards[layer_index] = (
            lax.psum_scatter(grads[0], ("dp", "blk"), scatter_dimension=0, tiled=True),
            lax.psum_scatter(grads[1], ("dp", "blk"), scatter_dimension=0, tiled=True),
            lax.psum_scatter(grads[2], ("dp", "blk"), scatter_dimension=0, tiled=True),
            lax.psum_scatter(grads[3], ("dp", "blk"), scatter_dimension=0, tiled=True),
            lax.psum_scatter(grads[4], ("dp", "blk"), scatter_dimension=0, tiled=True),
            lax.psum_scatter(grads[5], ("dp", "blk"), scatter_dimension=0, tiled=True),
            lax.psum_scatter(grads[6], ("dp", "blk"), scatter_dimension=0, tiled=True),
            lax.psum_scatter(grads[7], ("dp", "blk"), scatter_dimension=0, tiled=True),
            lax.psum_scatter(grads[8], ("dp", "blk"), scatter_dimension=0, tiled=True),
            lax.psum_scatter(grads[9], ("dp", "blk"), scatter_dimension=0, tiled=True),
            lax.psum_scatter(grads[10], ("dp", "blk"), scatter_dimension=0, tiled=True),
            lax.psum_scatter(grads[11], ("dp", "blk"), scatter_dimension=0, tiled=True),
            lax.psum_scatter(grads[12], ("dp", "blk"), scatter_dimension=0, tiled=True),
        )

    def head_tables(grad_plane):
        return (
            table_collect(bucket_line, grad_plane, line_count),
            table_collect(bucket_across, grad_plane, plane_count),
            table_collect(bucket_upward, grad_plane, plane_count),
        )

    line_terms, across_terms, upward_terms = lax.map(head_tables, score_total)
    grad_line, grad_across, grad_upward = lax.psum(
        (line_terms.T, across_terms.T, upward_terms.T), ("dp", "blk")
    )
    stacked = [
        jnp.stack([grad_shards[layer_index][member] for layer_index in range(layers)])
        for member in range(13)
    ]
    return (
        hidden_out,
        grad_state.astype(jnp.bfloat16),
        stacked[0],
        stacked[1],
        stacked[2],
        stacked[3],
        stacked[4],
        stacked[5],
        stacked[6],
        stacked[7],
        stacked[8],
        stacked[9],
        stacked[10],
        stacked[11],
        stacked[12],
        grad_line,
        grad_across,
        grad_upward,
    )


def solution(mesh):
    placed = (
        P(("dp", "blk"), None),
        P(("dp", "blk"), None),
        P("dp"),
        P(None, ("dp", "blk")),
        P(None, ("dp", "blk"), None),
        P(None, ("dp", "blk")),
        P(None, ("dp", "blk")),
        P(None, ("dp", "blk"), None),
        P(None, ("dp", "blk")),
        P(None, ("dp", "blk")),
        P(None, ("dp", "blk")),
        P(None, ("dp", "blk"), None),
        P(None, ("dp", "blk")),
        P(None, ("dp", "blk"), None),
        P(None, ("dp", "blk")),
        P(None, ("dp", "blk")),
        P(None, ("dp", "blk")),
        P(),
        P(),
        P(),
    )
    return jax.shard_map(
        on_device,
        mesh=mesh,
        in_specs=placed,
        out_specs=(
            P(("dp", "blk"), None),
            P(("dp", "blk"), None),
            P(None, ("dp", "blk"), None),
            P(None, ("dp", "blk")),
            P(None, ("dp", "blk")),
            P(None, ("dp", "blk"), None),
            P(None, ("dp", "blk")),
            P(None, ("dp", "blk")),
            P(None, ("dp", "blk")),
            P(None, ("dp", "blk"), None),
            P(None, ("dp", "blk")),
            P(None, ("dp", "blk"), None),
            P(None, ("dp", "blk")),
            P(None, ("dp", "blk")),
            P(None, ("dp", "blk")),
            P(),
            P(),
            P(),
        ),
        check_vma=False,
    )
```

profile of v0, /device:TPU:0, one launch (start us, length us, event | category | flops | bytes accessed | tf_op | source)
XLA Modules:
  0.0 1984.6 jit_solution(13233467806746418403)
XLA Ops:
  33.2 41.0 %all-reduce.37 = (bf16[3072]{0:T(1024)(128)(2,1)S(1)}, bf16[3072]{0:T(1024)(128)(2,1)S(1)}, bf16[768]{0:T(1024)(128)(2,1)S(1)}, bf16[768]{0:T(1024)(128)(2,1)S(1...) all-reduce(bf16[3072]{0:T(1024)(128)(2,1)S(1)} %dynamic-update-slic, ...), channel_id=23, replica_groups=mesh['dp'=16,'blk'=2] {'dp','blk'}, use_global_device_ids=true, to_apply=%add.14 | all-reduce | flops 18432 | bytes 73728
  86.9 154.2 %while.26 = (s32[]{:T(128)}, f32[12,256,512]{2,1,0:T(8,128)}, s32[12]{0:T(128)S(1)}, f32[32,12]{0,1:T(8,128)S(1)}, s32[256,512]{1,0:T(8,128)S(1)}, /*index=5*/f3...) while((s32[]{:T(128)}, f32[12,256,512]{2,1,0:T(8,128)}, ...), condition=%wide.region_4.5_spmd.clone, body=%wide.region_0.4_spmd.clone.sunk | while | flops 69206016 | bytes 5772355 | solution.py:342
  90.0 6.6 select_reduce_fusion.10
  102.8 6.6 select_reduce_fusion.10
  115.6 6.6 select_reduce_fusion.10
  128.4 6.6 select_reduce_fusion.10
  141.2 6.6 select_reduce_fusion.10
  154.0 6.6 select_reduce_fusion.10
  166.8 6.6 select_reduce_fusion.10
  179.6 6.6 select_reduce_fusion.10
  192.4 6.6 select_reduce_fusion.10
  205.2 6.6 select_reduce_fusion.10
  218.0 6.6 select_reduce_fusion.10
  230.8 6.6 select_reduce_fusion.10
  241.1 7.5 copy.124
  287.3 11.6 multiply_convert_fusion.3
  304.1 19.7 all-gather.43.cloned.1.call-done
  358.1 21.6 %all-gather.45.cloned.1.call-done = bf16[1,768,768]{2,1,0:T(8,128)(2,1)} async-done(((bf16[1,24,768]{2,1,0:T(8,128)(2,1)}), bf16[1,768,768]{2,1,0:T(8,128)(2,1)}) %all-gather.45.cloned.1.call-update) | async-done | bytes 1179664 | tf_op jit(solution)/shard_map/all_gather | solution.py:351
  381.9 63.3 %all-gather.47.cloned.1.call-done = bf16[1,768,3072]{2,1,0:T(8,128)(2,1)} async-done(((bf16[1,24,3072]{2,1,0:T(8,128)(2,1)}), bf16[1,768,3072]{2,1,0:T(8,128)(2,1)}) %all-gather.47.cloned.1.call-update) | async-done | bytes 4718608 | tf_op jit(solution)/shard_map/all_gather | solution.py:355
  445.2 12.0 multiply_convert_fusion.2
  457.2 53.4 %all-gather.49.cloned.1.call-done = bf16[1,3072,768]{2,1,0:T(8,128)(2,1)} async-done(((bf16[1,96,768]{2,1,0:T(8,128)(2,1)}), bf16[1,3072,768]{2,1,0:T(8,128)(2,1)}) %all-gather.49.cloned.1.call-update) | async-done | bytes 4718608 | tf_op jit(solution)/shard_map/all_gather | solution.py:357
  552.1 5.9 collective-permute-done.5
  585.1 208.4 %while.27 = (s32[]{:T(128)}, f32[12,32]{1,0:T(8,128)}, f32[12,64]{1,0:T(8,128)}, f32[12,64]{1,0:T(8,128)}, f32[12,256,512]{2,1,0:T(8,128)}, /*index=5*/s32[256,5...) while((s32[]{:T(128)}, f32[12,32]{1,0:T(8,128)}, ...), condition=%wide.region_79.80_spmd.clone, body=%wide.region_75.79_spmd.clone.sunk | while | flops 69336928 | bytes 4199429 | solution.py:400
  591.8 8.3 select_reduce_fusion.13
  609.1 8.3 select_reduce_fusion.13
  626.4 8.3 select_reduce_fusion.13
  643.7 8.3 select_reduce_fusion.13
  661.0 8.3 select_reduce_fusion.13
  678.3 8.3 select_reduce_fusion.13
  695.6 8.3 select_reduce_fusion.13
  712.9 8.3 select_reduce_fusion.13
  730.2 8.3 select_reduce_fusion.13
  747.5 8.3 select_reduce_fusion.13
  764.9 8.3 select_reduce_fusion.13
  782.2 8.3 select_reduce_fusion.13
  813.5 9.3 collective-permute-done.7
  827.6 8.1 copy.151
  837.3 5.2 fusion.230
  844.2 5.2 fusion.235
  867.9 84.0 %all-reduce.40.cloned.1.call-done = (f32[768]{0:T(1024)}, f32[768]{0:T(1024)}, f32[768]{0:T(1024)}, f32[768]{0:T(1024)}, f32[768]{0:T(1024)}, /*index=5*/f32[768...) async-done(((f32[768]{0:T(1024)}, f32[768]{0:T(1024)}, ...) | async-done | bytes 81424
  970.6 86.8 %reduce-scatter.15.cloned.1.call-done = f32[24,768]{1,0:T(8,128)} async-done(((f32[768,768]{1,0:T(8,128)}), f32[24,768]{1,0:T(8,128)}) %reduce-scatter.15.cloned.1.call-update) | async-done | bytes 73744 | tf_op jit(solution)/shard_map/reduce_scatter | solution.py:381
  1057.4 104.2 %reduce-scatter.13.cloned.1.call-done = f32[24,768]{1,0:T(8,128)} async-done(((f32[768,768]{1,0:T(8,128)}), f32[24,768]{1,0:T(8,128)}) %reduce-scatter.13.cloned.1.call-update) | async-done | bytes 73744 | tf_op jit(solution)/shard_map/reduce_scatter | solution.py:381
  1163.2 122.1 %reduce-scatter.27.cloned.1.call-done = f32[24,2304]{1,0:T(8,128)} async-done(((f32[768,2304]{1,0:T(8,128)}), f32[24,2304]{1,0:T(8,128)}) %reduce-scatter.27.cloned.1.call-update) | async-done | bytes 221200
  1286.9 123.3 %reduce-scatter.25.cloned.1.call-done = f32[24,2304]{1,0:T(8,128)} async-done(((f32[768,2304]{1,0:T(8,128)}), f32[24,2304]{1,0:T(8,128)}) %reduce-scatter.25.cloned.1.call-update) | async-done | bytes 221200
  1412.7 138.3 %reduce-scatter.19.cloned.1.call-done = f32[24,3072]{1,0:T(8,128)} async-done(((f32[768,3072]{1,0:T(8,128)}), f32[24,3072]{1,0:T(8,128)}) %reduce-scatter.19.cloned.1.call-update) | async-done | bytes 294928 | tf_op jit(solution)/shard_map/reduce_scatter | solution.py:385
  1551.0 141.4 %reduce-scatter.17.cloned.1.call-done = f32[24,3072]{1,0:T(8,128)} async-done(((f32[768,3072]{1,0:T(8,128)}), f32[24,3072]{1,0:T(8,128)}) %reduce-scatter.17.cloned.1.call-update) | async-done | bytes 294928 | tf_op jit(solution)/shard_map/reduce_scatter | solution.py:385
  1694.3 138.5 %reduce-scatter.23.cloned.1.call-done = f32[96,768]{1,0:T(8,128)} async-done(((f32[3072,768]{1,0:T(8,128)}), f32[96,768]{1,0:T(8,128)}) %reduce-scatter.23.cloned.1.call-update) | async-done | bytes 294928 | tf_op jit(solution)/shard_map/reduce_scatter | solution.py:387
  1832.8 141.4 %reduce-scatter.21.cloned.1.call-done = f32[96,768]{1,0:T(8,128)} async-done(((f32[3072,768]{1,0:T(8,128)}), f32[96,768]{1,0:T(8,128)}) %reduce-scatter.21.cloned.1.call-update) | async-done | bytes 294928 | tf_op jit(solution)/shard_map/reduce_scatter | solution.py:387
  (716 shorter events, 419.9 us)
Async XLA Ops:
  7.2 241.5 %all-gather.35.cloned.1.call-start = ((), (), s32[]{:S(2)}) async-start(), calls=%async_computation.14 | async-start | bytes 3649536 | tf_op jit(solution)/shard_map/all_gather | solution.py:348
  8.9 270.9 %all-gather.37.cloned.1.call-start = ((), (), s32[]{:S(2)}) async-start(), calls=%async_computation.15 | async-start | bytes 1216512 | tf_op jit(solution)/shard_map/all_gather | solution.py:351
  10.4 276.9 %all-gather.39.cloned.1.call-start = ((), (), s32[]{:S(2)}) async-start(), calls=%async_computation.16 | async-start | bytes 4866048 | tf_op jit(solution)/shard_map/all_gather | solution.py:355
  12.2 286.7 %all-gather.41.cloned.1.call-start = ((), (), s32[]{:S(2)}) async-start(), calls=%async_computation.17 | async-start | bytes 4866048 | tf_op jit(solution)/shard_map/all_gather | solution.py:357
  14.0 309.8 %all-gather.43.cloned.1.call-start = ((), (), s32[]{:S(2)}) async-start(), calls=%async_computation.18 | async-start | bytes 3649536 | tf_op jit(solution)/shard_map/all_gather | solution.py:348
  14.6 365.1 %all-gather.45.cloned.1.call-start = ((), (), s32[]{:S(2)}) async-start(), calls=%async_computation.19 | async-start | bytes 1216512 | tf_op jit(solution)/shard_map/all_gather | solution.py:351
  15.1 430.1 %all-gather.47.cloned.1.call-start = ((), (), s32[]{:S(2)}) async-start(), calls=%async_computation.20 | async-start | bytes 4866048 | tf_op jit(solution)/shard_map/all_gather | solution.py:355
  15.9 494.7 %all-gather.49.cloned.1.call-start = ((), (), s32[]{:S(2)}) async-start(), calls=%async_computation.21 | async-start | bytes 4866048 | tf_op jit(solution)/shard_map/all_gather | solution.py:357
  15.9 67.5 %collective-permute-start = (s32[2,256]{1,0:T(2,128)}, s32[2,256]{1,0:T(2,128)S(1)}, u32[]{:S(2)}, u32[]{:S(2)}) collective-permute-start(s32[2,256]{1,0:T(2,128)} %param.27), channel_id=1, source_target_pairs={{1,0},{0,1},{3,2},{2,3},{5,4},{4,5},{7,6},{6,7},{9,8},{8,9},{11,10... | collective-permute-start | bytes 6152 | tf_op jit(solution)/shard_map/ppermute | solution.py:19
  19.0 932.9 %all-reduce.40.cloned.1.call-start = ((), (), s32[]{:S(2)}) async-start(), calls=%async_computation.24 | async-start | bytes 229376
  79.9 219.0 %copy-start.67 = (f32[768]{0:T(1024)}, f32[768]{0:T(1024)S(1)}, u32[]{:S(2)}) copy-start(f32[768]{0:T(1024)S(1)} %convert_element_type.715) | copy-start | bytes 9220
  82.2 428.4 %copy-start.69 = (f32[768]{0:T(1024)}, f32[768]{0:T(1024)S(1)}, u32[]{:S(2)}) copy-start(f32[768]{0:T(1024)S(1)} %convert_element_type.724) | copy-start | bytes 9220
  254.6 12.5 collective-permute-start.1
  259.5 16.1 collective-permute-start.2
  281.8 17.2 copy-start.11
  303.3 23.7 %copy-start.9 = (f32[256,768]{1,0:T(8,128)}, f32[256,768]{1,0:T(8,128)S(1)}, u32[]{:S(2)}) copy-start(f32[256,768]{1,0:T(8,128)S(1)} %get-tuple-element.367) | copy-start | bytes 2359300
  303.3 23.7 %copy-start.80 = (f32[256]{0:T(256)}, f32[256]{0:T(256)S(1)}, u32[]{:S(2)}) copy-start(f32[256]{0:T(256)S(1)} %broadcast_multiply_fusion.2) | copy-start | bytes 3076
  329.7 12.5 collective-permute-start.3
  334.6 15.4 collective-permute-start.4
  357.4 22.3 %copy-start.10 = (f32[256,768]{1,0:T(8,128)S(1)}, f32[256,768]{1,0:T(8,128)}, u32[]{:S(2)}) copy-start(f32[256,768]{1,0:T(8,128)} %copy-done.9) | copy-start | bytes 2359300
  357.4 22.3 %copy-start.71 = (f32[768]{0:T(1024)S(1)}, f32[768]{0:T(1024)}, u32[]{:S(2)}) copy-start(f32[768]{0:T(1024)} %convert_element_type.718) | copy-start | bytes 9220
  357.4 22.3 %copy-start.77 = (f32[768]{0:T(1024)S(1)}, f32[768]{0:T(1024)}, u32[]{:S(2)}) copy-start(f32[768]{0:T(1024)} %convert_element_type.719) | copy-start | bytes 9220
  357.4 22.3 %copy-start.81 = (f32[256]{0:T(256)S(1)}, f32[256]{0:T(256)}, u32[]{:S(2)}) copy-start(f32[256]{0:T(256)} %copy-done.80) | copy-start | bytes 3076
  357.4 22.3 %copy-start.90 = (f32[256]{0:T(256)S(1)}, f32[256]{0:T(256)}, u32[]{:S(2)}) copy-start(f32[256]{0:T(256)} %fusion.223) | copy-start | bytes 3076
  357.4 22.3 %copy-start.116 = (f32[768]{0:T(1024)S(1)}, f32[768]{0:T(1024)}, u32[]{:S(2)}) copy-start(f32[768]{0:T(1024)} %convert_element_type.722) | copy-start | bytes 9220
  358.1 99.1 %copy-start.57 = (bf16[12,64,256]{2,1,0:T(8,128)(2,1)}, bf16[12,64,256]{2,1,0:T(8,128)(2,1)S(1)}, u32[]{:S(2)}) copy-start(bf16[12,64,256]{2,1,0:T(8,128)(2,1)S(1)} %fusion.133) | copy-start | bytes 1179652
  358.1 87.1 %copy-start.101 = (f32[3072]{0:T(1024)S(1)}, f32[3072]{0:T(1024)}, u32[]{:S(2)}) copy-start(f32[3072]{0:T(1024)} %convert_element_type.725) | copy-start | bytes 36868
  381.6 141.8 %copy-start.16 = (f32[256,768]{1,0:T(8,128)}, f32[256,768]{1,0:T(8,128)S(1)}, u32[]{:S(2)}) copy-start(f32[256,768]{1,0:T(8,128)S(1)} %get-tuple-element.373) | copy-start | bytes 2359300
  381.6 129.0 %copy-start.87 = (f32[256]{0:T(256)}, f32[256]{0:T(256)S(1)}, u32[]{:S(2)}) copy-start(f32[256]{0:T(256)S(1)} %broadcast_multiply_fusion.1) | copy-start | bytes 3076
  381.9 75.4 %copy-start.107 = (f32[256]{0:T(256)}, f32[256]{0:T(256)S(1)}, u32[]{:S(2)}) copy-start(f32[256]{0:T(256)S(1)} %multiply_reduce_fusion.11) | copy-start | bytes 3076
  381.9 128.7 %copy-start.98 = (f32[256]{0:T(256)}, f32[256]{0:T(256)S(1)}, u32[]{:S(2)}) copy-start(f32[256]{0:T(256)S(1)} %fusion.224) | copy-start | bytes 3076
  381.9 128.7 %copy-start.115 = (f32[768]{0:T(1024)S(1)}, f32[768]{0:T(1024)}, u32[]{:S(2)}) copy-start(f32[768]{0:T(1024)} %convert_element_type.726) | copy-start | bytes 9220
  537.9 12.3 collective-permute-start.6
  542.0 15.9 collective-permute-start.5
  550.1 14.4 copy-start.121
  579.5 218.5 %collective-permute-start.8 = (bf16[256,768]{0,1:T(8,128)(2,1)}, bf16[256,768]{0,1:T(8,128)(2,1)}, u32[]{:S(2)}, u32[]{:S(2)}) collective-permute-start(bf16[256,768]{0,1:T(8,128)(2,1)} %bitcast.68), channel_id=1, source_target_pairs={{1,0},{0,1},{3,2},{2,3},{5,4},{4,5},{7,6},{6,7},{9,8},{8,9},{11,10... | collective-permute-start | bytes 1179656 | tf_op jit(solution)/shard_map/ppermute | solution.py:19
  800.4 257.0 %reduce-scatter.15.cloned.1.call-start = ((), (), s32[]{:S(2)}) async-start(), calls=%async_computation.9 | async-start | bytes 2433024 | tf_op jit(solution)/shard_map/reduce_scatter | solution.py:381
  803.6 358.1 %reduce-scatter.13.cloned.1.call-start = ((), (), s32[]{:S(2)}) async-start(), calls=%async_computation.8 | async-start | bytes 2433024 | tf_op jit(solution)/shard_map/reduce_scatter | solution.py:381
  805.6 479.7 %reduce-scatter.27.cloned.1.call-start = ((), (), s32[]{:S(2)}) async-start(), calls=%async_computation.23 | async-start | bytes 7299072
  809.8 600.4 %reduce-scatter.25.cloned.1.call-start = ((), (), s32[]{:S(2)}) async-start(), calls=%async_computation.22 | async-start | bytes 7299072
  812.4 10.3 collective-permute-start.7
  835.7 715.3 %reduce-scatter.19.cloned.1.call-start = ((), (), s32[]{:S(2)}) async-start(), calls=%async_computation.11 | async-start | bytes 9732096 | tf_op jit(solution)/shard_map/reduce_scatter | solution.py:385
  842.6 849.8 %reduce-scatter.17.cloned.1.call-start = ((), (), s32[]{:S(2)}) async-start(), calls=%async_computation.10 | async-start | bytes 9732096 | tf_op jit(solution)/shard_map/reduce_scatter | solution.py:385
  849.4 983.4 %reduce-scatter.23.cloned.1.call-start = ((), (), s32[]{:S(2)}) async-start(), calls=%async_computation.13 | async-start | bytes 9732096 | tf_op jit(solution)/shard_map/reduce_scatter | solution.py:387
  855.9 1118.2 %reduce-scatter.21.cloned.1.call-start = ((), (), s32[]{:S(2)}) async-start(), calls=%async_computation.12 | async-start | bytes 9732096 | tf_op jit(solution)/shard_map/reduce_scatter | solution.py:387
  1286.9 689.1 %copy-start.111 = (f32[32,12]{0,1:T(8,128)S(1)}, f32[32,12]{0,1:T(8,128)}, u32[]{:S(2)}) copy-start(f32[32,12]{0,1:T(8,128)} %get-tuple-element.607) | copy-start | bytes 4612
  1286.9 689.7 %copy-start.110 = (f32[64,12]{0,1:T(8,128)S(1)}, f32[64,12]{0,1:T(8,128)}, u32[]{:S(2)}) copy-start(f32[64,12]{0,1:T(8,128)} %get-tuple-element.608) | copy-start | bytes 9220
  1286.9 690.3 %copy-start.109 = (f32[64,12]{0,1:T(8,128)S(1)}, f32[64,12]{0,1:T(8,128)}, u32[]{:S(2)}) copy-start(f32[64,12]{0,1:T(8,128)} %get-tuple-element.609) | copy-start | bytes 9220
  (111 other events, 416.3 us)
Sparse Core Ops, SparseCore 0:
  11.5 63.1 all-gather.34
  77.7 52.9 all-gather.36
  134.1 62.5 all-gather.38
  199.6 62.4 all-gather.40
  264.8 58.9 all-gather.42
  326.6 53.0 all-gather.44
  382.6 62.5 all-gather.46
  448.1 62.4 all-gather.48
  800.6 151.2 all-reduce.39
  957.0 100.3 reduce-scatter.14
  1063.5 98.0 reduce-scatter.12
  1167.1 118.0 reduce-scatter.26
  1291.9 118.2 reduce-scatter.24
  1416.0 134.9 reduce-scatter.18
  1557.7 134.5 reduce-scatter.16
  1698.1 134.6 reduce-scatter.22
  1839.5 134.5 reduce-scatter.20
where the time goes:
time: 2000 us; the launch traced here: 1980 us
  waiting for transfers between devices  1270 us (64%)
  other arithmetic  328 us (16%)
  local copies, waits for them, and re-layouts  161 us (8%)
  matrix products  135 us (7%)
  blocking collectives  41 us (2%)
  loops' own time  25.1 us (1%)
    unnamed x20, waiting for transfers between devices  331 us
    reduce_scatter x2, waiting for transfers between devices, on_device(): lax.psum_scatter(grads[9], ('dp', 'blk'), scatter_dimension=0, tiled=True)  280 us
    reduce_scatter x2, waiting for transfers between devices, on_device(): lax.psum_scatter(grads[7], ('dp', 'blk'), scatter_dimension=0, tiled=True)  280 us
    reduce_scatter x2, waiting for transfers between devices, on_device(): lax.psum_scatter(grads[3], ('dp', 'blk'), scatter_dimension=0, tiled=True)  191 us
    reduce_sum x24, other arithmetic, table_collect(): jnp.sum(jnp.where(codes[None] == code_range[:, None, None], grad_plane[No...  137 us
    reduce_sum x24, other arithmetic, table_lookup(): jnp.sum(jnp.where(codes[None] == code_range[:, None, None], column[:, Non...  99.8 us
    all_gather x2, waiting for transfers between devices, on_device(): lax.all_gather(in_weight[layer_index], ('dp', 'blk'), axis=0, tiled=True)  63.3 us
    all_gather x2, waiting for transfers between devices, on_device(): lax.all_gather(back_weight[layer_index], ('dp', 'blk'), axis=0, tiled=True)  53.4 us
  transfers between devices with their start and end apart: 26, of which 19 were waited for; matrix products, arithmetic and copies ran while one was open for 28% of the time, Pallas kernels for 0%

commit v1 on v0

v1 whole, which is shorter than its diff:
```python
import functools
import math

import jax
import jax.numpy as jnp
from jax import lax
from jax.experimental import pallas as pl
from jax.experimental.pallas import tpu as pltpu
from jax.sharding import PartitionSpec as P

REACH_1D = 128
REACH_2D = 256
COORD_TOP = 1000

eps_norm = 1e-12
big_negative = -1e30

BF = jnp.bfloat16
F4 = jnp.float32
AXES = ("dp", "blk")
VMEM = 56 * 1024 * 1024

HEAD = 64
QUAD = 256
LANES = 128


def bucket_marks(bucket_count, far_reach):
    half_count = bucket_count // 2
    exact_limit = half_count // 2
    thresholds = []
    for bucket_step in range(1, half_count):
        if bucket_step < exact_limit:
            thresholds.append(bucket_step)
        else:
            thresholds.append(
                math.ceil(
                    exact_limit
                    * (far_reach / exact_limit)
                    ** ((bucket_step - exact_limit) / (half_count - exact_limit))
                )
            )
    return thresholds


def params(**more):
    return pltpu.CompilerParams(vmem_limit_bytes=VMEM, **more)


def cost(flops, traffic):
    return pl.CostEstimate(flops=int(flops), bytes_accessed=int(traffic), transcendentals=0)


def mm(left, right):
    return jnp.dot(left, right, preferred_element_type=F4)


def mm_t(left, right):
    return lax.dot_general(left, right, (((1,), (1,)), ((), ())), preferred_element_type=F4)


def pick(table_row, codes):
    return jnp.take_along_axis(
        jnp.broadcast_to(table_row, codes.shape), codes, axis=1, mode="promise_in_bounds"
    )


def bias_kernel(heads, line_n, plane_n, scal, own_ref, keys_ref, plane_ref, line_ref, out_ref):
    rows = out_ref.shape[1]
    chunk = 32
    step = pl.program_id(0)
    length, half = scal[0], scal[1]
    magnitude = lax.broadcasted_iota(jnp.int32, (1, LANES), 1)

    def marks(base, count, reach):
        code = jnp.zeros((1, LANES), jnp.int32)
        for mark in bucket_marks(count, reach):
            code = code + (magnitude + base >= mark).astype(jnp.int32)
        return code

    near, far = marks(0, plane_n, REACH_2D), marks(LANES, plane_n, REACH_2D)
    flat = marks(0, line_n, REACH_1D)
    key_index = step * LANES + magnitude
    key_place = jnp.where(
        key_index < rows, half * rows + key_index, (1 - half) * rows + key_index - rows
    )
    live = key_place < length
    across_key, upward_key = keys_ref[0:1, :], keys_ref[1:2, :]

    def plane_code(offset):
        size = jnp.minimum(jnp.abs(offset), 2 * LANES - 1)
        low = jnp.bitwise_and(size, LANES - 1)
        code = jnp.where(size >= LANES, pick(far, low), pick(near, low))
        return code + jnp.where(offset > 0, plane_n // 2, 0)

    def body(index, carry):
        first = pl.multiple_of(index * chunk, chunk)
        span = pl.ds(first, chunk)
        across = plane_code(across_key - own_ref[span, 0:1])
        upward = plane_code(upward_key - own_ref[span, 1:2]) + plane_n
        place = (
            half * rows + first + lax.broadcasted_iota(jnp.int32, (chunk, LANES), 0)
        )
        offset = key_place - place
        along = pick(flat, jnp.minimum(jnp.abs(offset), LANES - 1)) + jnp.where(
            offset > 0, line_n // 2, 0
        )
        for head in range(heads):
            plane_row = plane_ref[head : head + 1, :]
            total = (
                pick(line_ref[head : head + 1, :], along)
                + pick(plane_row, across)
                + pick(plane_row, upward)
            )
            out_ref[head, span, :] = jnp.where(live, total, big_negative)
        return carry

    lax.fori_loop(0, rows // chunk, body, 0)


def score_biases(length, half, own_xy, key_xy, line_table, across_table, upward_table):
    heads = line_table.shape[1]
    rows, keys = own_xy.shape[1], key_xy.shape[1]
    line_n, plane_n = line_table.shape[0], across_table.shape[0]
    plane = jnp.concatenate([across_table, upward_table], axis=0).astype(F4).T
    line = jnp.pad(line_table.astype(F4).T, ((0, 0), (0, LANES - line_n)))
    whole = pl.BlockSpec(memory_space=pltpu.VMEM)
    return pl.pallas_call(
        functools.partial(bias_kernel, heads, line_n, plane_n),
        grid=(keys // LANES,),
        in_specs=[
            pl.BlockSpec(memory_space=pltpu.SMEM),
            whole,
            pl.BlockSpec((2, LANES), lambda j: (0, j)),
            whole,
            whole,
        ],
        out_specs=pl.BlockSpec((heads, rows, LANES), lambda j: (0, 0, j)),
        out_shape=jax.ShapeDtypeStruct((heads, rows, keys), F4),
        compiler_params=params(),
        cost_estimate=cost(3e9, heads * rows * keys * 4),
        name="score_bias",
    )(jnp.stack([length, half]), own_xy.T, key_xy, plane, line)


def head_masks(dtype):
    lane = lax.broadcasted_iota(jnp.int32, (1, QUAD), 1)
    return [
        ((lane >= h * HEAD) & (lane < (h + 1) * HEAD)).astype(dtype) for h in range(QUAD // HEAD)
    ]


def attn_fwd_kernel(x_ref, wq, wk, wv, bq, bv, bias_ref, q_out, k_out, v_out, p_out, o_out):
    rows = q_out.shape[0]
    x = x_ref[...]
    q = ((mm(x[:rows], wq[...]) + bq[...]) * 0.125).astype(BF)
    k = mm(x, wk[...]).astype(BF)
    v = (mm(x, wv[...]) + bv[...]).astype(BF)
    q_out[...] = q
    k_out[...] = k
    v_out[...] = v
    lane = lax.broadcasted_iota(jnp.int32, (rows, QUAD), 1)
    mixed = jnp.zeros((rows, QUAD), F4)
    for h, mask in enumerate(head_masks(BF)):
        s = mm_t(q * mask, k) + bias_ref[h]
        e = jnp.exp(s - jnp.max(s, axis=-1, keepdims=True))
        p = (e * (1.0 / jnp.sum(e, axis=-1, keepdims=True))).astype(BF)
        p_out[h] = p
        mixed = jnp.where(
            (lane >= h * HEAD) & (lane < (h + 1) * HEAD), mm(p, v), mixed
        )
    o_out[...] = mixed.astype(BF)


def attn_fwd(x_all, packed, bq, bv, bias):
    keys, width = x_all.shape
    heads, rows, _ = bias.shape
    quads = width // QUAD
    per = QUAD // HEAD
    weight = lambda base: pl.BlockSpec((width, QUAD), lambda j: (0, base * quads + j))
    vec = pl.BlockSpec((1, QUAD), lambda j: (0, j))
    cols = lambda n: pl.BlockSpec((n, QUAD), lambda j: (0, j))
    scores = pl.BlockSpec((per, rows, keys), lambda j: (j, 0, 0))
    sds = jax.ShapeDtypeStruct
    return pl.pallas_call(
        attn_fwd_kernel,
        grid=(quads,),
        in_specs=[
            pl.BlockSpec((keys, width), lambda j: (0, 0)),
            weight(0),
            weight(1),
            weight(2),
            vec,
            vec,
            scores,
        ],
        out_specs=[cols(rows), cols(keys), cols(keys), scores, cols(rows)],
        out_shape=[
            sds((rows, width), BF),
            sds((keys, width), BF),
            sds((keys, width), BF),
            sds((heads, rows, keys), BF),
            sds((rows, width), BF),
        ],
        compiler_params=params(),
        cost_estimate=cost(5e9, 16e6),
        name="attention_forward",
    )(x_all, packed, packed, packed, bq, bv, bias)


def normed(values):
    centered = values - jnp.mean(values, axis=-1, keepdims=True)
    variance = jnp.mean(centered * centered, axis=-1, keepdims=True)
    scale = lax.rsqrt(variance + eps_norm)
    return centered * scale, scale


def ffn_fwd_kernel(
    x_ref, o_ref, wo, win, wback, bo, g1, s1, bin_, bb, g2, s2,
    r1_out, h_out, act_out, slope_out, r2_out, x_out, low_out, middle, total,
):
    step = pl.program_id(0)

    @pl.when(step == 0)
    def _():
        r1 = x_ref[...].astype(F4) + mm(o_ref[...], wo[...]) + bo[...]
        r1_out[...] = r1
        n, _ = normed(r1)
        h = n * g1[...] + s1[...]
        middle[...] = h
        h_out[...] = h.astype(BF)
        total[...] = jnp.zeros_like(total)

    u = mm(h_out[...], win[...]) + bin_[...]
    cdf = 0.5 * (1.0 + lax.erf(u * 0.7071067811865476))
    act = (u * cdf).astype(BF)
    act_out[...] = act
    slope_out[...] = (cdf + u * (0.3989422804014327 * jnp.exp(-0.5 * u * u))).astype(BF)
    total[...] += mm(act, wback[...])

    @pl.when(step == pl.num_programs(0) - 1)
    def _():
        r2 = middle[...] + total[...] + bb[...]
        r2_out[...] = r2
        n, _ = normed(r2)
        x = n * g2[...] + s2[...]
        x_out[...] = x
        low_out[...] = x.astype(BF)


def ffn_fwd(x, o, packed, back, vecs):
    rows, width = x.shape
    ff = back.shape[0]
    parts = ff // width
    full = pl.BlockSpec((rows, width), lambda j: (0, 0))
    vec = pl.BlockSpec((1, width), lambda j: (0, 0))
    chunk = pl.BlockSpec((rows, width), lambda j: (0, j))
    sds = jax.ShapeDtypeStruct
    bo, g1, s1, bin_, bb, g2, s2 = vecs
    return pl.pallas_call(
        ffn_fwd_kernel,
        grid=(parts,),
        in_specs=[
            full,
            full,
            pl.BlockSpec((width, width), lambda j: (0, 3)),
            pl.BlockSpec((width, width), lambda j: (0, 4 + j)),
            pl.BlockSpec((width, width), lambda j: (j, 0)),
            vec, vec, vec,
            pl.BlockSpec((1, width), lambda j: (0, j)),
            vec, vec, vec,
        ],
        out_specs=[full, full, chunk, chunk, full, full, full],
        out_shape=[
            sds((rows, width), F4),
            sds((rows, width), BF),
            sds((rows, ff), BF),
            sds((rows, ff), BF),
            sds((rows, width), F4),
            sds((rows, width), F4),
            sds((rows, width), BF),
        ],
        scratch_shapes=[pltpu.VMEM((rows, width), F4), pltpu.VMEM((rows, width), F4)],
        compiler_params=params(),
        cost_estimate=cost(5e9, 20e6),
        name="dense_forward",
    )(x, o, packed, packed, back, bo, g1, s1, bin_, bb, g2, s2)


def norm_back(grad, values, gain):
    n, scale = normed(values)
    e = grad * gain
    inner = jnp.mean(e * n, axis=-1, keepdims=True)
    out = (e - jnp.mean(e, axis=-1, keepdims=True) - n * inner) * scale
    return out, jnp.sum(grad * n, axis=0, keepdims=True), jnp.sum(grad, axis=0, keepdims=True)


def ffn_bwd_kernel(
    own_ref, far_ref, r2_ref, g2, wback, slope, win, r1_ref, g1, wo,
    df_out, du_out, dr1_out, db_out, do_out, vec_out, binv_out, dr2, total,
):
    step = pl.program_id(0)

    @pl.when(step == 0)
    def _():
        grad = own_ref[...] + far_ref[...].astype(F4)
        out, gain, shift = norm_back(grad, r2_ref[...], g2[...])
        dr2[...] = out
        low = out.astype(BF)
        df_out[...] = low
        vec_out[3:4, :] = jnp.sum(low.astype(F4), axis=0, keepdims=True)
        vec_out[4:5, :] = gain
        vec_out[5:6, :] = shift
        total[...] = jnp.zeros_like(total)

    du = (mm_t(df_out[...], wback[...]) * slope[...].astype(F4)).astype(BF)
    du_out[...] = du
    binv_out[...] = jnp.sum(du.astype(F4), axis=0, keepdims=True)
    total[...] += mm_t(du, win[...])

    @pl.when(step == pl.num_programs(0) - 1)
    def _():
        out, gain, shift = norm_back(dr2[...] + total[...], r1_ref[...], g1[...])
        dr1_out[...] = out
        low = out.astype(BF)
        db_out[...] = low
        vec_out[0:1, :] = jnp.sum(low.astype(F4), axis=0, keepdims=True)
        vec_out[1:2, :] = gain
        vec_out[2:3, :] = shift
        do_out[...] = mm_t(low, wo[...]).astype(BF)


def ffn_bwd(own, far, r2, g2, back, slope, packed, r1, g1):
    rows, width = own.shape
    ff = back.shape[0]
    parts = ff // width
    full = pl.BlockSpec((rows, width), lambda j: (0, 0))
    vec = pl.BlockSpec((1, width), lambda j: (0, 0))
    chunk = pl.BlockSpec((rows, width), lambda j: (0, j))
    sds = jax.ShapeDtypeStruct
    return pl.pallas_call(
        ffn_bwd_kernel,
        grid=(parts,),
        in_specs=[
            full, full, full, vec,
            pl.BlockSpec((width, width), lambda j: (j, 0)),
            chunk,
            pl.BlockSpec((width, width), lambda j: (0, 4 + j)),
            full, vec,
            pl.BlockSpec((width, width), lambda j: (0, 3)),
        ],
        out_specs=[
            full, chunk, full, full, full,
            pl.BlockSpec((8, width), lambda j: (0, 0)),
            pl.BlockSpec((1, width), lambda j: (0, j)),
        ],
        out_shape=[
            sds((rows, width), BF),
            sds((rows, ff), BF),
            sds((rows, width), F4),
            sds((rows, width), BF),
            sds((rows, width), BF),
            sds((8, width), F4),
            sds((1, ff), F4),
        ],
        scratch_shapes=[pltpu.VMEM((rows, width), F4), pltpu.VMEM((rows, width), F4)],
        compiler_params=params(),
        cost_estimate=cost(5e9, 20e6),
        name="dense_backward",
    )(own, far, r2, g2, back, slope, packed, r1, g1, packed)


def attn_bwd_kernel(
    q_ref, k_ref, v_ref, p_ref, do_ref, wq, wk, wv, dr1_ref,
    dq_out, dk_out, dv_out, ds_out, own_out, far_out, vec_out, far_sum,
):
    step = pl.program_id(0)
    rows = q_ref.shape[0]

    @pl.when(step == 0)
    def _():
        own_out[...] = dr1_ref[...]
        far_sum[...] = jnp.zeros_like(far_sum)

    q, k, v, do = q_ref[...], k_ref[...], v_ref[...], do_ref[...]
    q_t, do_t = q.T, do.T
    lane = lax.broadcasted_iota(jnp.int32, (rows, QUAD), 1)
    dq = jnp.zeros((rows, QUAD), F4)
    dk_t, dv_t = [], []
    for h, mask in enumerate(head_masks(BF)):
        low = p_ref[h]
        p = low.astype(F4)
        t = p * mm_t(do * mask, v)
        ds = (t - p * jnp.sum(t, axis=-1, keepdims=True)).astype(BF)
        ds_out[h] = ds
        dq = jnp.where((lane >= h * HEAD) & (lane < (h + 1) * HEAD), mm(ds, k), dq)
        dk_t.append(mm(q_t[h * HEAD : (h + 1) * HEAD], ds))
        dv_t.append(mm(do_t[h * HEAD : (h + 1) * HEAD], low))
    dk = jnp.concatenate(dk_t, axis=0).T.astype(BF)
    dv = jnp.concatenate(dv_t, axis=0).T.astype(BF)
    dq = (dq.astype(BF).astype(F4) * 0.125).astype(BF)
    dq_out[...] = dq
    dk_out[...] = dk
    dv_out[...] = dv
    vec_out[0:1, :] = jnp.sum(dq.astype(F4), axis=0, keepdims=True)
    vec_out[1:2, :] = jnp.sum(dv.astype(F4), axis=0, keepdims=True)
    both = mm_t(dk, wk[...]) + mm_t(dv, wv[...])
    own_out[...] += mm_t(dq, wq[...]) + both[:rows]
    far_sum[...] += both[rows:]

    @pl.when(step == pl.num_programs(0) - 1)
    def _():
        far_out[...] = far_sum[...].astype(BF)


def attn_bwd(q, k, v, p, do, packed, dr1):
    heads, rows, keys = p.shape
    width = q.shape[1]
    quads = width // QUAD
    per = QUAD // HEAD
    weight = lambda base: pl.BlockSpec((width, QUAD), lambda j: (0, base * quads + j))
    cols = lambda n: pl.BlockSpec((n, QUAD), lambda j: (0, j))
    scores = pl.BlockSpec((per, rows, keys), lambda j: (j, 0, 0))
    full = pl.BlockSpec((rows, width), lambda j: (0, 0))
    sds = jax.ShapeDtypeStruct
    return pl.pallas_call(
        attn_bwd_kernel,
        grid=(quads,),
        in_specs=[
            cols(rows), cols(keys), cols(keys), scores, cols(rows),
            weight(0), weight(1), weight(2), full,
        ],
        out_specs=[
            cols(rows), cols(keys), cols(keys), scores, full, full,
            pl.BlockSpec((8, QUAD), lambda j: (0, j)),
        ],
        out_shape=[
            sds((rows, width), BF),
            sds((keys, width), BF),
            sds((keys, width), BF),
            sds((heads, rows, keys), BF),
            sds((rows, width), F4),
            sds((rows, width), BF),
            sds((8, width), F4),
        ],
        scratch_shapes=[pltpu.VMEM((rows, width), F4)],
        compiler_params=params(),
        cost_estimate=cost(8e9, 20e6),
        name="attention_backward",
    )(q, k, v, p, do, packed, packed, packed, dr1)


def wgrad_kernel(x_ref, dq, dk, dv, o_ref, db, h_ref, du, out_ref, x_t, h_t):
    step = pl.program_id(0)
    rows = o_ref.shape[0]

    @pl.when(step == 0)
    def _():
        x_t[...] = x_ref[...].T
        out_ref[...] = mm(x_t[:, :rows], dq[...]).astype(BF)

    @pl.when(step == 1)
    def _():
        out_ref[...] = mm(x_t[...], dk[...]).astype(BF)

    @pl.when(step == 2)
    def _():
        out_ref[...] = mm(x_t[...], dv[...]).astype(BF)

    @pl.when(step == 3)
    def _():
        h_t[...] = h_ref[...].T
        out_ref[...] = mm(o_ref[...].T, db[...]).astype(BF)

    @pl.when(step > 3)
    def _():
        out_ref[...] = mm(h_t[...], du[...]).astype(BF)


def wgrad(x_all, dq, dk, dv, o, db, h, du, columns):
    keys, width = x_all.shape
    rows, ff = du.shape
    parts = ff // width
    full = pl.BlockSpec((rows, width), lambda j: (0, 0))
    both = pl.BlockSpec((keys, width), lambda j: (0, 0))
    return pl.pallas_call(
        wgrad_kernel,
        grid=(4 + parts,),
        in_specs=[
            both, full, both, both, full, full, full,
            pl.BlockSpec((rows, width), lambda j: (0, jnp.maximum(j - 4, 0))),
        ],
        out_specs=pl.BlockSpec((width, width), lambda j: (0, j)),
        out_shape=jax.ShapeDtypeStruct((width, columns), BF),
        scratch_shapes=[pltpu.VMEM((width, keys), BF), pltpu.VMEM((width, rows), BF)],
        compiler_params=params(),
        cost_estimate=cost(4e9, 15e6),
        name="weight_gradients",
    )(x_all, dq, dk, dv, o, db, h, du)


def wgrad_back_kernel(own_rows, act, df, _, out_ref):
    width = df.shape[1]
    grad = mm(act[...].T, df[...])
    parts = out_ref.shape[1] // width
    grad = grad.reshape(grad.shape[0] // (own_rows * parts), parts, own_rows, width)
    for part in range(parts):
        out_ref[:, part * width : (part + 1) * width] = (
            grad[:, part].reshape(out_ref.shape[0], width).astype(BF)
        )


def wgrad_back(act, df, packed_grad, own_rows):
    rows, ff = act.shape
    width = df.shape[1]
    parts = ff // width
    return pl.pallas_call(
        functools.partial(wgrad_back_kernel, own_rows),
        grid=(parts,),
        in_specs=[
            pl.BlockSpec((rows, width), lambda j: (0, j)),
            pl.BlockSpec((rows, width), lambda j: (0, 0)),
            pl.BlockSpec(memory_space=pl.ANY),
        ],
        out_specs=pl.BlockSpec((width // parts, ff), lambda j: (j, 2)),
        out_shape=jax.ShapeDtypeStruct(packed_grad.shape, BF),
        input_output_aliases={2: 0},
        compiler_params=params(),
        cost_estimate=cost(2e9, 8e6),
        name="weight_gradients_back",
    )(act, df, packed_grad)


def edge_row(count, reach):
    half = count // 2
    marks = bucket_marks(count, reach)
    lane = lax.broadcasted_iota(jnp.int32, (1, LANES), 1)
    edges = jnp.full((1, LANES), -(1 << 20), jnp.int32)
    for k, mark in enumerate(marks):
        edges = jnp.where(lane == k, 1 - mark, edges)
        edges = jnp.where(lane == half - 1 + k, mark, edges)
    return jnp.where(lane == 2 * half - 2, 1 << 20, edges)


def tables_kernel(
    line_n, plane_n, keys_ref, own_ref, one_ref, two_ref, out_ref, steps, line_steps, spots
):
    keys, rows = keys_ref.shape[0], own_ref.shape[0]
    span = steps.shape[2]

    @pl.when(pl.program_id(0) == 0)
    def _():
        place = lax.broadcasted_iota(jnp.int32, (keys, span), 1)
        for plane in range(2):
            steps[plane] = (keys_ref[:, plane : plane + 1] < place).astype(F4).astype(BF)
            spots[plane] = jnp.clip(
                own_ref[:, plane : plane + 1] + edge_row(plane_n, REACH_2D), 0, COORD_TOP + 1
            )
        line_place = lax.broadcasted_iota(jnp.int32, (keys, keys), 1)
        line_steps[...] = (keys_ref[:, 2:3] <= line_place).astype(F4).astype(BF)
        spots[2] = jnp.clip(own_ref[:, 2:3] + edge_row(line_n, REACH_1D), 0, keys) - 1

    one, two = one_ref[0], two_ref[0]

    def collect(sums, spot):
        safe = jnp.maximum(spot, 0)
        low = jnp.bitwise_and(safe, LANES - 1)
        block = lax.shift_right_logical(safe, 7)
        found = jnp.zeros(spot.shape, F4)
        for b in range(sums.shape[1] // LANES):
            piece = jnp.take_along_axis(
                sums[:, b * LANES : (b + 1) * LANES], low, axis=1, mode="promise_in_bounds"
            )
            found = jnp.where(block == b, piece, found)
        return jnp.sum(jnp.where(spot >= 0, found, 0.0), axis=0, keepdims=True)

    for plane in range(2):
        sums = mm(one, steps[plane]) + mm(two, steps[plane])
        out_ref[0, plane : plane + 1, :] = collect(sums, spots[plane])
    sums = mm(one, line_steps[...]) + mm(two, line_steps[...])
    out_ref[0, 2:3, :] = collect(sums, spots[2])


def table_sums(key_columns, own_columns, one, two, line_n, plane_n):
    heads, rows, keys = one.shape
    span = -(-(COORD_TOP + 2) // LANES) * LANES
    whole = pl.BlockSpec(memory_space=pltpu.VMEM)
    scores = pl.BlockSpec((1, rows, keys), lambda j: (j, 0, 0))
    return pl.pallas_call(
        functools.partial(tables_kernel, line_n, plane_n),
        grid=(heads,),
        in_specs=[whole, whole, scores, scores],
        out_specs=pl.BlockSpec((1, 8, LANES), lambda j: (j, 0, 0)),
        out_shape=jax.ShapeDtypeStruct((heads, 8, LANES), F4),
        scratch_shapes=[
            pltpu.VMEM((2, keys, span), BF),
            pltpu.VMEM((keys, keys), BF),
            pltpu.VMEM((3, rows, LANES), jnp.int32),
        ],
        compiler_params=params(),
        cost_estimate=cost(16e9, 6e6),
        name="table_sums",
    )(key_columns, own_columns, one, two)


def buckets_from_sums(sums, count):
    half = count // 2
    below, above = sums[:, : half - 1], sums[:, half - 1 : 2 * half - 2]
    total = sums[:, 2 * half - 2 : 2 * half - 1]
    zero = jnp.zeros_like(total)
    lower = jnp.concatenate([above[:, :1], below], axis=1) - jnp.concatenate([below, zero], axis=1)
    upper = jnp.concatenate([above[:, 1:], total], axis=1) - above
    return jnp.concatenate([lower, zero, upper], axis=1).T


def exchange(block, devices, distance):
    return lax.ppermute(block, AXES, [(i, i ^ distance) for i in range(devices)])


def summed_everywhere(block, devices):
    distance = 1
    while distance < devices:
        block = block + exchange(block, devices, distance)
        distance *= 2
    return block


def on_device(
    devices,
    hidden_in, cotangent, lengths, coords,
    qkv_weight, query_bias, value_bias, out_weight, out_bias, norm1_gain, norm1_shift,
    in_weight, in_bias, back_weight, back_bias, norm2_gain, norm2_shift,
    line_table, horizontal_table, vertical_table,
):
    rows, width = hidden_in.shape
    layers, own_rows, _ = qkv_weight.shape
    ff = in_weight.shape[2]
    parts = ff // width
    line_n, plane_n = line_table.shape[0], horizontal_table.shape[0]
    half = lax.axis_index("blk")
    me = lax.axis_index(AXES)
    length = lengths[0]
    flip = lambda block: exchange(block, devices, 1)

    columns = 3 * width + width + 2 * ff
    vec_list = []
    for l in range(layers):
        vec_list += [query_bias[l], value_bias[l], out_bias[l], norm1_gain[l], norm1_shift[l]]
        vec_list += [in_bias[l, g * own_rows : (g + 1) * own_rows] for g in range(parts)]
        vec_list += [back_bias[l], norm2_gain[l], norm2_shift[l]]
    vec_count = len(vec_list) // layers
    vec_block = jnp.pad(jnp.stack(vec_list, axis=1), ((0, 0), (0, LANES - len(vec_list))))

    gathered = []
    for l in range(layers):
        pieces = [qkv_weight[l], out_weight[l], in_weight[l]]
        pieces += [back_weight[l, g * own_rows : (g + 1) * own_rows] for g in range(parts)]
        if l == 0:
            pieces.append(vec_block)
        gathered.append(
            lax.all_gather(jnp.concatenate(pieces, axis=1), AXES, axis=0, tiled=True)
        )

    far_x = flip(hidden_in)
    far_coords = flip(coords)
    key_coords = jnp.concatenate([coords, far_coords], axis=1)
    bias = score_biases(
        length, half, coords, key_coords, line_table, horizontal_table, vertical_table
    )

    vec_rows = gathered[0][:, columns : columns + len(vec_list)].astype(F4).T

    def vec_of(l, k):
        return vec_rows[l * vec_count + k][None, :]

    def in_bias_of(l):
        part = vec_rows[l * vec_count + 5 : l * vec_count + 5 + parts]
        return part.reshape(parts, devices, own_rows).transpose(1, 0, 2).reshape(1, ff)

    def back_of(l):
        part = gathered[l][:, columns - ff : columns].reshape(devices, own_rows, parts, width)
        return part.transpose(0, 2, 1, 3).reshape(ff, width)

    backs = [back_of(l) for l in range(layers)]
    state, low = hidden_in, hidden_in
    saved = []
    for l in range(layers):
        if l > 0:
            far_x = flip(low)
        x_all = jnp.concatenate([low, far_x], axis=0)
        q, k, v, p, o = attn_fwd(x_all, gathered[l], vec_of(l, 0), vec_of(l, 1), bias)
        r1, h, act, slope, r2, state, low = ffn_fwd(
            state, o, gathered[l], backs[l],
            (
                vec_of(l, 2), vec_of(l, 3), vec_of(l, 4), in_bias_of(l),
                vec_of(l, 5 + parts), vec_of(l, 6 + parts), vec_of(l, 7 + parts),
            ),
        )
        saved.append((x_all, q, k, v, p, o, r1, h, act, slope, r2))
    hidden_out = low

    place = half * rows + jnp.arange(rows, dtype=jnp.int32)
    own = jnp.where((place < length)[:, None], cotangent.astype(F4), 0.0)
    far = jnp.zeros((rows, width), BF)
    shards = [None] * layers
    vec_grads = [None] * layers
    score_grads = []
    for l in reversed(range(layers)):
        x_all, q, k, v, p, o, r1, h, act, slope, r2 = saved[l]
        df, du, dr1, db, do, vec_a, vec_in = ffn_bwd(
            own, far, r2, vec_of(l, 6 + parts), backs[l], slope, gathered[l], r1, vec_of(l, 3)
        )
        dq, dk, dv, ds, own, far_part, vec_b = attn_bwd(q, k, v, p, do, gathered[l], dr1)
        far = flip(far_part)
        packed = wgrad(x_all, dq, dk, dv, o, db, h, du, columns)
        packed = wgrad_back(act, df, packed, own_rows)
        shards[l] = lax.psum_scatter(packed, AXES, scatter_dimension=0, tiled=True).astype(F4)
        score_grads.append(ds)
        vec_grads[l] = jnp.concatenate(
            [vec_b[0:2], vec_a[0:3], vec_in.reshape(parts, width), vec_a[3:6]], axis=0
        )
    grad_in = (own + far.astype(F4)).astype(BF)

    other = (1 - half) * rows + jnp.arange(rows, dtype=jnp.int32)
    key_columns = jnp.concatenate(
        [key_coords, jnp.concatenate([place, other])[None]], axis=0
    ).T
    own_columns = jnp.concatenate([coords, place[None]], axis=0).T
    sums = table_sums(key_columns, own_columns, score_grads[0], score_grads[1], line_n, plane_n)
    heads = sums.shape[0]
    flat = jnp.concatenate(vec_grads + [sums[:, :3].reshape(-1, width)], axis=0)
    flat = summed_everywhere(flat, devices)
    sums = flat[layers * vec_count :].reshape(heads, 3, LANES)
    grad_across = buckets_from_sums(sums[:, 0], plane_n)
    grad_upward = buckets_from_sums(sums[:, 1], plane_n)
    grad_line = buckets_from_sums(sums[:, 2], line_n)

    vec_grad = flat[: layers * vec_count].reshape(layers, vec_count, width)
    mine = lax.dynamic_slice_in_dim(vec_grad, me * own_rows, own_rows, axis=2)
    wide = vec_grad[:, 5 : 5 + parts].reshape(layers, ff)
    grad_in_bias = lax.dynamic_slice_in_dim(wide, me * parts * own_rows, parts * own_rows, axis=1)
    rest = lambda k: mine[:, k]

    shard = jnp.stack(shards)
    grad_qkv = shard[:, :, : 3 * width]
    grad_out = shard[:, :, 3 * width : 4 * width]
    grad_inw = shard[:, :, 4 * width : 4 * width + ff]
    grad_back = (
        shard[:, :, 4 * width + ff :]
        .reshape(layers, own_rows, parts, width)
        .transpose(0, 2, 1, 3)
        .reshape(layers, parts * own_rows, width)
    )
    return (
        hidden_out, grad_in,
        grad_qkv, rest(0), rest(1), grad_out, rest(2), rest(3), rest(4),
        grad_inw, grad_in_bias, grad_back, rest(5 + parts), rest(6 + parts), rest(7 + parts),
        grad_line, grad_across, grad_upward,
    )


def solution(mesh):
    devices = mesh.shape["dp"] * mesh.shape["blk"]
    tokens = P(AXES, None)
    weight = P(None, AXES, None)
    vector = P(None, AXES)
    return jax.shard_map(
        functools.partial(on_device, devices),
        mesh=mesh,
        in_specs=(
            tokens, tokens, P("dp"), P(None, AXES),
            weight, vector, vector, weight, vector, vector, vector,
            weight, vector, weight, vector, vector, vector,
            P(), P(), P(),
        ),
        out_specs=(
            tokens, tokens,
            weight, vector, vector, weight, vector, vector, vector,
            weight, vector, weight, vector, vector, vector,
            P(), P(), P(),
        ),
        check_vma=False,
    )
```

time: 2000 us -> 691 us (0.35)
  waiting for transfers between devices: 1270 us -> 373 us
  other arithmetic: 328 us -> 12 us
  Pallas kernels: 0 us -> 167 us
  matrix products: 135 us -> 0 us
  local copies, waits for them, and re-layouts: 161 us -> 101 us
  blocking collectives: 41 us -> 0 us
  loops' own time: 25.1 us -> 0 us
    reduce_scatter x6 -> x2, waiting for transfers between devices: 751 us -> 217 us  [on_device(): lax.psum_scatter(packed, AXES, scatter_dimension=0, tiled=True).astype(F4)]
    unnamed x20 -> x4, waiting for transfers between devices: 331 us -> 0.74 us
    reduce_sum x65 -> x0, other arithmetic: 252 us -> none  [the longest x24 137 us: table_collect(): jnp.sum(jnp.where(codes[None] == code_range[:, None, None], grad_plane[No...]
    pallas_call x0 -> x14, Pallas kernels: none -> 167 us  [the longest x1 25.1 us: table_sums(): pl.pallas_call(functools.partial(tables_kernel, line_n, plane_n), grid=(h...]
    dot_general x41 -> x0, matrix products: 131 us -> none  [the longest x7 29.4 us: over_rows(): lax.dot_general(left, right, (((0,), (0,)), ((), ())), preferred_element_...]
    dynamic_update_slice x36 -> x0, local copies, waits for them, and re-layouts: 46.3 us -> none  [on_device(): line_terms, across_terms, upward_terms = lax.map(head_tables, score_total)]
    unnamed x1 -> x0, blocking collectives: 41 us -> none
    all_gather x8 -> x2, waiting for transfers between devices: 158 us -> 123 us  [on_device(): lax.all_gather(jnp.concatenate(pieces, axis=1), AXES, axis=0, tiled=True)]
  transfers between devices with their start and end apart: 26 -> 14, of which waited for: 19 -> 11; matrix products, arithmetic and copies ran while one was open for 28% -> 13% of each run, Pallas kernels for 0% -> 16%
where the time goes in v1:
time: 691 us; the launch traced here: 679 us
  waiting for transfers between devices  373 us (54%)
  Pallas kernels  167 us (24%)
  local copies, waits for them, and re-layouts  101 us (15%)
  between operations  15 us (2%)
  other arithmetic  12 us (2%)
  starting transfers between devices  10.5 us (2%)
    reduce_scatter x2, waiting for transfers between devices, on_device(): lax.psum_scatter(packed, AXES, scatter_dimension=0, tiled=True).astype(F4)  217 us
    all_gather x2, waiting for transfers between devices, on_device(): lax.all_gather(jnp.concatenate(pieces, axis=1), AXES, axis=0, tiled=True)  123 us
    ppermute x10, waiting for transfers between devices, exchange(): lax.ppermute(block, AXES, [(i, i ^ distance) for i in range(devices)])  32.7 us
    pallas_call x1, Pallas kernels, table_sums(): pl.pallas_call(functools.partial(tables_kernel, line_n, plane_n), grid=(h...  25.1 us
    pallas_call x2, Pallas kernels, attn_bwd(): pl.pallas_call(attn_bwd_kernel, grid=(quads,), in_specs=[cols(rows), cols...  25 us
    pallas_call x2, Pallas kernels, ffn_bwd(): pl.pallas_call(ffn_bwd_kernel, grid=(parts,), in_specs=[full, full, full,...  23.2 us
    pallas_call x2, Pallas kernels, ffn_fwd(): pl.pallas_call(ffn_fwd_kernel, grid=(parts,), in_specs=[full, full, pl.Bl...  22.2 us
    pallas_call x1, Pallas kernels, score_biases(): pl.pallas_call(functools.partial(bias_kernel, heads, line_n, plane_n), gr...  21.4 us
  transfers between devices with their start and end apart: 14, of which 11 were waited for; matrix products, arithmetic and copies ran while one was open for 13% of the time, Pallas kernels for 16%

profile of v1, /device:TPU:0, one launch (start us, length us, event | category | flops | bytes accessed | tf_op | source)
XLA Modules:
  0.0 678.6 jit_solution(16645892474697959567)
XLA Ops:
  24.2 3.0 collective-permute-start
  28.6 1.3 pad_convert_fusion.line_ref
  29.9 1.4 convert_bitcast_fusion.1.plane_ref
  32.9 1.5 copy.175
  34.4 2.3 collective-permute-done.1
  37.3 21.4 %score_bias.1.bias_ref = f32[12,256,512]{2,1,0:T(8,128)} custom-call(s32[2]{0:T(128)} %pad_add_fusion.3.scal, s32[256,2]{1,0:T(8,128)} %bitcast.153, s32[2,512]{1,0:T(2,128)} %copy-done.17, f32[12,128]{1,0:T(8,128)} %convert_bitcast_fusion.1.plane_ref, f32[12,128]{1,0:T(8,128)} %pad_convert_fusion.line_ref), custom_call_target="tpu_custom_call" | custom-call | flops 3000000000 | bytes 6291456 | tf_op jit(solution)/shard_map/score_bias/pallas_call | solution.py:128
  58.7 71.5 %all-gather.3.cloned.1.call-done.wq.wk.wv.wo.win = bf16[768,9344]{1,0:T(8,128)(2,1)} async-done(((bf16[24,9344]{1,0:T(8,128)(2,1)}), bf16[768,9344]{1,0:T(8,128)(2,1)}) %all-gather.3.cloned.1.call-update) | async-done | bytes 14352400 | tf_op jit(solution)/shard_map/all_gather | solution.py:661
  131.2 3.4 fusion.8
  134.7 1.7 copy.176.bq
  136.4 1.7 copy.177.bv
  138.1 5.0 slice.406
  143.1 9.8 %reshape.96 = bf16[32,24,4,768]{3,2,1,0:T(4,128)(2,1)} reshape(bf16[768,3072]{1,0:T(8,128)(2,1)} %slice.406) | data formatting | bytes 9437184 | tf_op jit(solution)/shard_map/reshape | solution.py:681
  152.9 5.5 copy.178
  158.3 1.7 copy.180.bo
  160.1 1.8 copy.181.g1
  161.8 1.7 copy.182.s1
  164.7 1.2 copy.179
  166.7 1.7 copy.183.bb
  169.9 9.3 %attention_forward.2 = (bf16[256,768]{1,0:T(8,128)(2,1)}, bf16[512,768]{1,0:T(8,128)(2,1)}, bf16[512,768]{1,0:T(8,128)(2,1)}, bf16[12,256,512]{2,1,0:T(8,128)(2,1)}, bf16[256,768]{1,0:T(8,128)(2,1)}) custom-call(bf16[512,768]{1,0:T(8,128)(2,1)} %copy-done, bf16[768,9344]{1,0:T(8,128)(2,1)} %all-gather.3.cloned.1.call-done.wq.wk.wv.wo.win, ...), custom_call_target="tpu_custom_call" | custom-call | flops 5000000000 | bytes 16000000 | tf_op jit(solution)/shard_map/attention_forward/pallas_call | solution.py:185
  179.2 11.1 %dense_forward.2 = (f32[256,768]{1,0:T(8,128)}, bf16[256,768]{1,0:T(8,128)(2,1)}, bf16[256,3072]{1,0:T(8,128)(2,1)}, bf16[256,3072]{1,0:T(8,128)(2,1)}, f32[256,...) custom-call(bf16[256,768]{1,0:T(8,128)(2,1)} %x_ref.1, bf16[256,768]{1,0:T(8,128)(2,1)} %get-tuple-element.69.o_ref, ...), custom_call_target="tpu_custom_call" | custom-call | flops 5000000000 | bytes 20000000 | tf_op jit(solution)/shard_map/dense_forward/pallas_call | solution.py:260
  192.5 51.1 %all-gather.5.cloned.1.call-done.wq.wk.wv.wo.win = bf16[768,9216]{1,0:T(8,128)(2,1)} async-done(((bf16[24,9216]{1,0:T(8,128)(2,1)}), bf16[768,9216]{1,0:T(8,128)(2,1)}) %all-gather.5.cloned.1.call-update) | async-done | bytes 14155792 | tf_op jit(solution)/shard_map/all_gather | solution.py:661
  243.6 4.8 slice.416
  248.4 9.8 %reshape.100 = bf16[32,24,4,768]{3,2,1,0:T(4,128)(2,1)} reshape(bf16[768,3072]{1,0:T(8,128)(2,1)} %slice.416) | data formatting | bytes 9437184 | tf_op jit(solution)/shard_map/reshape | solution.py:681
  258.2 5.5 copy.188
  273.5 9.7 %attention_forward.3 = (bf16[256,768]{1,0:T(8,128)(2,1)}, bf16[512,768]{1,0:T(8,128)(2,1)}, bf16[512,768]{1,0:T(8,128)(2,1)}, bf16[12,256,512]{2,1,0:T(8,128)(2,1)}, bf16[256,768]{1,0:T(8,128)(2,1)}) custom-call(bf16[512,768]{1,0:T(8,128)(2,1)} %copy-done.1, bf16[768,9216]{1,0:T(8,128)(2,1)} %all-gather.5.cloned.1.call-done.wq.wk.wv.wo.win, ...), custom_call_target="tpu_custom_call" | custom-call | flops 5000000000 | bytes 16000000 | tf_op jit(solution)/shard_map/attention_forward/pallas_call | solution.py:185
  283.2 11.0 %dense_forward.3 = (f32[256,768]{1,0:T(8,128)}, bf16[256,768]{1,0:T(8,128)(2,1)}, bf16[256,3072]{1,0:T(8,128)(2,1)}, bf16[256,3072]{1,0:T(8,128)(2,1)}, f32[256,...) custom-call(f32[256,768]{1,0:T(8,128)} %get-tuple-element.70.x_ref, ...), custom_call_target="tpu_custom_call" | custom-call | flops 5000000000 | bytes 20000000 | tf_op jit(solution)/shard_map/dense_forward/pallas_call | solution.py:260
  295.1 11.2 %dense_backward.2 = (bf16[256,768]{1,0:T(8,128)(2,1)}, bf16[256,3072]{1,0:T(8,128)(2,1)}, f32[256,768]{1,0:T(8,128)}, bf16[256,768]{1,0:T(8,128)(2,1)}, bf16[256...) custom-call(f32[256,768]{1,0:T(8,128)} %convert_select_fusion.own_ref, ...), custom_call_target="tpu_custom_call" | custom-call | flops 5000000000 | bytes 20000000 | tf_op jit(solution)/shard_map/dense_backward/pallas_call | solution.py:341
  306.3 12.7 %attention_backward.2 = (bf16[256,768]{1,0:T(8,128)(2,1)}, bf16[512,768]{1,0:T(8,128)(2,1)}, bf16[512,768]{1,0:T(8,128)(2,1)}, bf16[12,256,512]{2,1,0:T(8,128)(2...) custom-call(bf16[256,768]{1,0:T(8,128)(2,1)} %get-tuple-element.78.q_ref, ...), custom_call_target="tpu_custom_call" | custom-call | flops 8000000000 | bytes 20000000 | tf_op jit(solution)/shard_map/attention_backward/pallas_call | solution.py:426
  319.0 10.2 %weight_gradients.3._ = bf16[768,9216]{1,0:T(8,128)(2,1)} custom-call(bf16[512,768]{1,0:T(8,128)(2,1)} %copy-done.1, bf16[256,768]{1,0:T(8,128)(2,1)} %get-tuple-element.106.dq, bf16[512,768]{1,0:T(8,128)(2,1)} %get-tuple-element.107.dk, bf16[512,768]{1,0:T(8,128)(2,1)} %get-tuple-element.108.dv, bf16[256,768]{1,0:T(8,128)(2,1)} %get-tuple-element.72.o_ref, ...), custom_call_target="tpu_custom_call" | custom-call | flops 4000000000 | bytes 15000000 | tf_op jit(solution)/shard_map/weight_gradients/pallas_call | solution.py:486
  329.2 5.3 weight_gradients_back.3
  336.0 10.7 %collective-permute-done.3.far_ref = bf16[256,768]{1,0:T(8,128)(2,1)S(1)} collective-permute-done((bf16[256,768]{1,0:T(8,128)(2,1)S(1)}, bf16[256,768]{1,0:T(8,128)(2,1)S(1)}, u32[]{:S(2)}, u32[]{:S(2)}) %collective-permute-start.3) | collective-permute-done | bytes 393248 | tf_op jit(solution)/shard_map/ppermute | solution.py:617
  347.5 12.0 %dense_backward.3 = (bf16[256,768]{1,0:T(8,128)(2,1)}, bf16[256,3072]{1,0:T(8,128)(2,1)}, f32[256,768]{1,0:T(8,128)}, bf16[256,768]{1,0:T(8,128)(2,1)}, bf16[256...) custom-call(f32[256,768]{1,0:T(8,128)} %get-tuple-element.87.own_ref, bf16[256,768]{1,0:T(8,128)(2,1)} %copy-done.10, ...), custom_call_target="tpu_custom_call" | custom-call | flops 5000000000 | bytes 20000000 | tf_op jit(solution)/shard_map/dense_backward/pallas_call | solution.py:341
  359.4 12.4 %attention_backward.3 = (bf16[256,768]{1,0:T(8,128)(2,1)}, bf16[512,768]{1,0:T(8,128)(2,1)}, bf16[512,768]{1,0:T(8,128)(2,1)}, bf16[12,256,512]{2,1,0:T(8,128)(2...) custom-call(bf16[256,768]{1,0:T(8,128)(2,1)} %get-tuple-element.74.q_ref, ...), custom_call_target="tpu_custom_call" | custom-call | flops 8000000000 | bytes 20000000 | tf_op jit(solution)/shard_map/attention_backward/pallas_call | solution.py:426
  371.8 10.4 %weight_gradients.2._ = bf16[768,9216]{1,0:T(8,128)(2,1)} custom-call(bf16[512,768]{1,0:T(8,128)(2,1)} %copy-done, bf16[256,768]{1,0:T(8,128)(2,1)} %get-tuple-element.98.dq, bf16[512,768]{1,0:T(8,128)(2,1)} %get-tuple-element.99.dk, bf16[512,768]{1,0:T(8,128)(2,1)} %get-tuple-element.100.dv, bf16[256,768]{1,0:T(8,128)(2,1)} %get-tuple-element.69.o_ref, ...), custom_call_target="tpu_custom_call" | custom-call | flops 4000000000 | bytes 15000000 | tf_op jit(solution)/shard_map/weight_gradients/pallas_call | solution.py:486
  382.2 5.2 weight_gradients_back.2
  392.5 25.1 %table_sums.1 = f32[12,8,128]{2,1,0:T(8,128)} custom-call(s32[512,3]{1,0:T(8,128)} %bitcast.151, s32[256,3]{1,0:T(8,128)} %bitcast.152, bf16[12,256,512]{2,1,0:T(8,128)(2,1)} %get-tuple-element.118.one_ref, bf16[12,256,512]{2,1,0:T(8,128)(2,1)} %get-tuple-element.119.two_ref), custom_call_target="tpu_custom_call" | custom-call | flops 16000000000 | bytes 6000000 | tf_op jit(solution)/shard_map/table_sums/pallas_call | solution.py:589
  420.1 1.5 collective-permute-start.5
  421.6 4.0 collective-permute-done.5
  425.7 1.3 collective-permute-done.6
  427.0 1.5 collective-permute-start.7
  428.6 5.9 collective-permute-done.7
  435.0 4.2 collective-permute-done.8
  439.2 1.4 collective-permute-start.9
  441.5 4.2 collective-permute-done.9
  449.1 49.6 %reduce-scatter.5.cloned.1.call-done = bf16[24,9216]{1,0:T(8,128)(2,1)} async-done(((bf16[768,9216]{1,0:T(8,128)(2,1)}), bf16[24,9216]{1,0:T(8,128)(2,1)}) %reduce-scatter.5.cloned.1.call-update) | async-done | bytes 442384 | tf_op jit(solution)/shard_map/reduce_scatter | solution.py:717
  498.8 167.5 %reduce-scatter.3.cloned.1.call-done = bf16[24,9216]{1,0:T(8,128)(2,1)} async-done(((bf16[768,9216]{1,0:T(8,128)(2,1)}), bf16[24,9216]{1,0:T(8,128)(2,1)}) %reduce-scatter.3.cloned.1.call-update) | async-done | bytes 442384 | tf_op jit(solution)/shard_map/reduce_scatter | solution.py:717
  666.3 1.3 maximum_convert_fusion
  667.5 1.5 maximum_convert_fusion.1
  (182 shorter events, 54.5 us)
Async XLA Ops:
  7.2 123.1 %all-gather.3.cloned.1.call-start = ((), (), s32[]{:S(2)}) async-start(), calls=%async_computation.2 | async-start | bytes 14800896 | tf_op jit(solution)/shard_map/all_gather | solution.py:661
  22.5 1.0 copy-start.9
  22.6 0.8 copy-start.8
  23.4 220.2 %all-gather.5.cloned.1.call-start = ((), (), s32[]{:S(2)}) async-start(), calls=%async_computation.3 | async-start | bytes 14598144 | tf_op jit(solution)/shard_map/all_gather | solution.py:661
  24.2 474.6 %reduce-scatter.5.cloned.1.call-start = ((), (), s32[]{:S(2)}) async-start(), calls=%async_computation.5 | async-start | bytes 14598144 | tf_op jit(solution)/shard_map/reduce_scatter | solution.py:717
  24.2 34.5 %collective-permute-start = (bf16[256,768]{1,0:T(8,128)(2,1)}, bf16[256,768]{1,0:T(8,128)(2,1)S(1)}, u32[]{:S(2)}, u32[]{:S(2)}) collective-permute-start(bf16[256,768]{1,0:T(8,128)(2,1)} %x_ref.1), channel_id=1, source_target_pairs={{0,1},{1,0},{2,3},{3,2},{4,5},{5,4},{6,7},{7,6},{8,9},{9,8},{10,11... | collective-permute-start | bytes 1179656 | tf_op jit(solution)/shard_map/ppermute | solution.py:617
  27.2 9.5 %collective-permute-start.1 = (s32[2,256]{1,0:T(2,128)}, s32[2,256]{1,0:T(2,128)S(1)}, u32[]{:S(2)}, u32[]{:S(2)}) collective-permute-start(s32[2,256]{1,0:T(2,128)} %param.23), channel_id=1, source_target_pairs={{0,1},{1,0},{2,3},{3,2},{4,5},{5,4},{6,7},{7,6},{8,9},{9,8},{10,11... | collective-permute-start | bytes 6152 | tf_op jit(solution)/shard_map/ppermute | solution.py:617
  36.7 0.6 copy-start.17
  58.7 76.0 %copy-start = (bf16[512,768]{1,0:T(8,128)(2,1)}, bf16[512,768]{1,0:T(8,128)(2,1)S(1)}, u32[]{:S(2)}) copy-start(bf16[512,768]{1,0:T(8,128)(2,1)S(1)} %constant_dynamic-update-slice_fusion.x_ref) | copy-start | bytes 2359300
  152.9 15.6 %copy-start.5 = (f32[1,768]{0,1:T(8,128)S(1)}, f32[1,768]{0,1:T(8,128)}, u32[]{:S(2)}) copy-start(f32[1,768]{0,1:T(8,128)} %get-tuple-element.131) | copy-start | bytes 9220
  152.9 16.3 %copy-start.4 = (f32[1,768]{0,1:T(8,128)S(1)}, f32[1,768]{0,1:T(8,128)}, u32[]{:S(2)}) copy-start(f32[1,768]{0,1:T(8,128)} %get-tuple-element.130) | copy-start | bytes 9220
  179.2 12.2 %copy-start.11 = (bf16[256,768]{1,0:T(8,128)(2,1)S(1)}, bf16[256,768]{1,0:T(8,128)(2,1)}, u32[]{:S(2)}) copy-start(bf16[256,768]{1,0:T(8,128)(2,1)} %param.21) | copy-start | bytes 1179652
  190.4 81.2 %collective-permute-start.2 = (bf16[256,768]{1,0:T(8,128)(2,1)}, bf16[256,768]{1,0:T(8,128)(2,1)}, u32[]{:S(2)}, u32[]{:S(2)}) collective-permute-start(bf16[256,768]{1,0:T(8,128)(2,1)} %get-tuple-element.71), channel_id=1, source_target_pairs={{0,1},{1,0},{2,3},{3,2},{4,5},{5,4},{6,7},{7,6},{8,9},{9,8},{10,11... | collective-permute-start | bytes 1179656 | tf_op jit(solution)/shard_map/ppermute | solution.py:617
  258.2 5.5 copy-start.3
  258.2 6.2 copy-start.2
  258.2 9.1 %copy-start.6 = (f32[4,768]{0,1:T(8,128)S(1)}, f32[4,768]{0,1:T(8,128)}, u32[]{:S(2)}) copy-start(f32[4,768]{0,1:T(8,128)} %get-tuple-element.138) | copy-start | bytes 36868
  272.6 0.9 copy-start.1
  334.5 1.0 copy-start.22
  334.5 331.8 %reduce-scatter.3.cloned.1.call-start = ((), (), s32[]{:S(2)}) async-start(), calls=%async_computation.4 | async-start | bytes 14598144 | tf_op jit(solution)/shard_map/reduce_scatter | solution.py:717
  335.5 11.3 %collective-permute-start.3 = (bf16[256,768]{1,0:T(8,128)(2,1)S(1)}, bf16[256,768]{1,0:T(8,128)(2,1)S(1)}, u32[]{:S(2)}, u32[]{:S(2)}) collective-permute-start(bf16[256,768]{1,0:T(8,128)(2,1)S(1)} %copy-done.22), channel_id=1, source_target_pairs={{0,1},{1,0},{2,3},{3,2},{4,5},{5,4},{6,7},{7,6},{8,9},{9,8},{10,11... | collective-permute-start | bytes 1179656 | tf_op jit(solution)/shard_map/ppermute | solution.py:617
  346.7 0.7 copy-start.10
  387.4 0.7 copy-start.14
  387.4 1.5 copy-start.18
  387.4 3.6 copy-start.15
  387.4 4.3 copy-start.12
  387.4 4.4 copy-start.21
  391.8 48.9 %collective-permute-start.4 = (bf16[256,768]{1,0:T(8,128)(2,1)S(1)}, bf16[256,768]{1,0:T(8,128)(2,1)S(1)}, u32[]{:S(2)}, u32[]{:S(2)}) collective-permute-start(bf16[256,768]{1,0:T(8,128)(2,1)S(1)} %copy-done.21), channel_id=1, source_target_pairs={{0,1},{1,0},{2,3},{3,2},{4,5},{5,4},{6,7},{7,6},{8,9},{9,8},{10,11... | collective-permute-start | bytes 1179656 | tf_op jit(solution)/shard_map/ppermute | solution.py:617
  392.4 25.1 %copy-start.13 = (f32[8,768]{1,0:T(8,128)S(1)}, f32[8,768]{1,0:T(8,128)}, u32[]{:S(2)}) copy-start(f32[8,768]{1,0:T(8,128)} %get-tuple-element.113) | copy-start | bytes 73732
  392.4 25.9 %copy-start.16 = (f32[1,3072]{1,0:T(1,128)S(1)}, f32[1,3072]{1,0:T(1,128)}, u32[]{:S(2)}) copy-start(f32[1,3072]{1,0:T(1,128)} %get-tuple-element.114) | copy-start | bytes 36868
  392.4 48.2 %copy-start.7 = (f32[256,768]{1,0:T(8,128)S(1)}, f32[256,768]{1,0:T(8,128)}, u32[]{:S(2)}) copy-start(f32[256,768]{1,0:T(8,128)} %get-tuple-element.94) | copy-start | bytes 2359300
  392.4 54.3 %copy-start.20 = (pred[16]{0:T(512)(128)(4,1)S(1)}, pred[16]{0:T(512)(128)(4,1)}, u32[]{:S(2)}) copy-start(pred[16]{0:T(512)(128)(4,1)} %constant.36.clone.1) | copy-start | bytes 52
  392.5 55.9 %copy-start.19 = (pred[32]{0:T(512)(128)(4,1)S(1)}, pred[32]{0:T(512)(128)(4,1)}, u32[]{:S(2)}) copy-start(pred[32]{0:T(512)(128)(4,1)} %constant.37.clone.1) | copy-start | bytes 100
  420.1 5.5 collective-permute-start.5
  425.7 1.4 collective-permute-start.6
  427.0 7.5 %collective-permute-start.7 = (f32[30,768]{1,0:T(8,128)S(1)}, f32[30,768]{1,0:T(8,128)S(1)}, u32[]{:S(2)}, u32[]{:S(2)}) collective-permute-start(f32[30,768]{1,0:T(8,128)S(1)} %add.70), channel_id=1, source_target_pairs={{0,4},{1,5},{2,6},{3,7},{4,0},{5,1},{6,2},{7,3},{8,12},{9,13},{10,... | collective-permute-start | bytes 276488 | tf_op jit(solution)/shard_map/ppermute | solution.py:617
  434.5 4.7 collective-permute-start.8
  439.2 6.5 collective-permute-start.9
Sparse Core Ops, SparseCore 0:
  23.5 106.6 all-gather.2
  133.8 109.7 all-gather.4
  334.6 164.1 reduce-scatter.4
  504.6 161.6 reduce-scatter.2
